TPU v7x, 32 devices: a whole 2x2x4 slice. The times are simulated.
32 devices in a mesh: dp: 8 (over z, y), expert: 4 (over x, core).
Axes of the slice: x: 2, y: 2, z: 4, core: 2. Of those that a mesh axis runs over, the one named last changes fastest.
Arguments:
- tokens: bfloat16 [65536, 512], P(('dp', 'expert')), may hold values from -6 to 6
- seq_lengths: int32 [32], P(('dp', 'expert')), may hold values from 256 to 2048, as said below
- group_map: int32 [32, 2048], P(('dp', 'expert')), may hold values from 0 to 2047, each once within a row
- gain_attn: bfloat16 [512], P(('dp', 'expert')), may hold values from 0.099609375 to 1.8984375
- gain_mix: bfloat16 [512], P(('dp', 'expert')), may hold values from 0.099609375 to 1.8984375
- w_qkv: bfloat16 [512, 1536], P(('dp', 'expert')), may hold values from -0.25 to 0.25
- w_out: bfloat16 [512, 512], P(('dp', 'expert')), may hold values from -2 to 2
- w_ctrl: bfloat16 [512, 16], P(('dp', 'expert')), may hold values from -0.125 to 0.125
- w_up: bfloat16 [16, 512, 2048], P('expert'), may hold values from -1 to 1
- w_down: bfloat16 [16, 2048, 512], P('expert'), may hold values from -2 to 2
- cotangent: bfloat16 [65536, 512], P(('dp', 'expert')), may hold values from -6 to 6
Outputs:
- output: bfloat16 [65536, 512], P(('dp', 'expert'))
- grad_tokens: bfloat16 [65536, 512], P(('dp', 'expert'))
- grad_gain_attn: float32 [512], P(('dp', 'expert'))
- grad_gain_mix: float32 [512], P(('dp', 'expert'))
- grad_w_qkv: float32 [512, 1536], P(('dp', 'expert'))
- grad_w_out: float32 [512, 512], P(('dp', 'expert'))
- grad_w_ctrl: float32 [512, 16], P(('dp', 'expert'))
- grad_w_up: float32 [16, 512, 2048], P('expert', 'dp')
- grad_w_down: float32 [16, 2048, 512], P('expert', 'dp')
Inputs may be any that keep to these rules, and one draw needn't show every extreme that they name: `seq_lengths`: each entry is 256 or 2048: that device's block of tokens is sequences of that length laid end to end; both values occur in every draw. `group_map`: each row is a permutation of 0 to 2047.
All inputs are finite; a program needn't handle non-finite values.
Results may differ from a plain program's by a relative error of at most 0.019.
Values may be sent and summed in bfloat16 or wider, within the bound.
No kernel may reach another device: no remote copies, remote signals or barrier semaphores. Data moves between devices by JAX's collectives and lax.ppermute only.
A program may use at most 320 MiB of HBM per device.

v0:
```python
import jax
import jax.numpy as jnp
from jax import lax
from jax.sharding import PartitionSpec as P

HEADS = 8
G = 32


eps_norm = 1e-05
masked_value = -1e30
root_half = 0.7071067811865476
density_norm = 0.3989422804014327


def rms_scale(values):
    return lax.rsqrt(jnp.mean(values * values, axis=-1, keepdims=True) + eps_norm)


def gelu_slope(values):
    cdf_part = 0.5 * (1.0 + lax.erf(values * root_half))
    return cdf_part + values * jnp.exp(-0.5 * values * values) * density_norm


def allowed_pairs(query_pos, key_pos, length):
    same_doc = query_pos[:, None] // length == key_pos[None, :] // length
    return same_doc & (key_pos[None, :] <= query_pos[:, None])


def split_parts(qkv_low, head_count):
    tok_rows, triple = qkv_low.shape
    feat_width = triple // 3
    head_size = feat_width // head_count
    queries = qkv_low[:, :feat_width].reshape(tok_rows, head_count, head_size)
    key_rows = qkv_low[:, feat_width : 2 * feat_width].reshape(tok_rows, head_count, head_size)
    value_rows = qkv_low[:, 2 * feat_width :].reshape(tok_rows, head_count, head_size)
    return (queries, key_rows, value_rows)


def block_scores(queries, key_rows, row_start, block_rows, length):
    tok_rows, head_count, head_size = key_rows.shape
    query_block = lax.dynamic_slice_in_dim(queries, row_start, block_rows, 0)
    scores = jnp.einsum(
        "qhd,khd->hqk", query_block, key_rows, preferred_element_type=jnp.float32
    ) * head_size ** (-0.5)
    query_pos = row_start + jnp.arange(block_rows, dtype=jnp.int32)
    key_pos = jnp.arange(tok_rows, dtype=jnp.int32)
    allowed = allowed_pairs(query_pos, key_pos, length)
    return (query_block, jnp.where(allowed[None], scores, masked_value))


def attend_forward(queries, key_rows, value_rows, length):
    tok_rows, head_count, head_size = queries.shape
    block_rows = min(tok_rows, 512)
    block_count = tok_rows // block_rows

    def one_block(block_index):
        row_start = block_index * block_rows
        query_block, scores = block_scores(queries, key_rows, row_start, block_rows, length)
        peak_score = jnp.max(scores, axis=-1, keepdims=True)
        exp_scores = jnp.exp(scores - peak_score)
        total = jnp.sum(exp_scores, axis=-1, keepdims=True)
        probs_low = (exp_scores / total).astype(jnp.bfloat16)
        mixed_rows = jnp.einsum(
            "hqk,khd->qhd", probs_low, value_rows, preferred_element_type=jnp.float32
        )
        return (mixed_rows.astype(jnp.bfloat16), (peak_score + jnp.log(total))[:, :, 0])

    outputs, log_totals = lax.map(one_block, jnp.arange(block_count, dtype=jnp.int32))
    return (outputs.reshape(tok_rows, head_count * head_size), log_totals)


def attend_backward(queries, key_rows, value_rows, log_totals, grad_attended, length):
    tok_rows, head_count, head_size = queries.shape
    block_rows = min(tok_rows, 512)
    block_count = tok_rows // block_rows
    score_scale = head_size ** (-0.5)
    grad_heads = grad_attended.reshape(tok_rows, head_count, head_size)

    def one_block(totals, block_index):
        grad_keys, grad_values = totals
        row_start = block_index * block_rows
        query_block, scores = block_scores(queries, key_rows, row_start, block_rows, length)
        probs = jnp.exp(scores - log_totals[block_index][:, :, None])
        probs_low = probs.astype(jnp.bfloat16)
        grad_block = lax.dynamic_slice_in_dim(grad_heads, row_start, block_rows, 0)
        grad_values = grad_values + jnp.einsum(
            "hqk,qhd->khd", probs_low, grad_block, preferred_element_type=jnp.float32
        )
        grad_probs = jnp.einsum(
            "qhd,khd->hqk", grad_block, value_rows, preferred_element_type=jnp.float32
        )
        row_total = jnp.sum(probs * grad_probs, axis=-1, keepdims=True)
        grad_scores = (probs * (grad_probs - row_total)).astype(jnp.bfloat16)
        grad_queries = (
            jnp.einsum("hqk,khd->qhd", grad_scores, key_rows, preferred_element_type=jnp.float32)
            * score_scale
        )
        grad_keys = (
            grad_keys
            + jnp.einsum(
                "hqk,qhd->khd", grad_scores, query_block, preferred_element_type=jnp.float32
            )
            * score_scale
        )
        return ((grad_keys, grad_values), grad_queries)

    zeros_heads = jnp.zeros((tok_rows, head_count, head_size), jnp.float32)
    (grad_keys, grad_values), grad_queries = lax.scan(
        one_block, (zeros_heads, zeros_heads), jnp.arange(block_count, dtype=jnp.int32)
    )
    feat_width = head_count * head_size
    joined = jnp.concatenate(
        [
            grad_queries.reshape(tok_rows, feat_width),
            grad_keys.reshape(tok_rows, feat_width),
            grad_values.reshape(tok_rows, feat_width),
        ],
        axis=1,
    )
    return joined.astype(jnp.bfloat16)


def norm_backward(grad_normed, source, scale_rows, gain_values):
    weighted = gain_values * grad_normed
    grad_gain = jnp.sum(grad_normed * source * scale_rows, axis=0)
    grad_source = scale_rows * weighted - source * scale_rows**3 * jnp.mean(
        weighted * source, axis=-1, keepdims=True
    )
    return (grad_gain, grad_source)


def on_device(
    tokens,
    seq_lengths,
    group_map,
    gain_attn,
    gain_mix,
    w_qkv,
    w_out,
    w_ctrl,
    w_up,
    w_down,
    cotangent,
):
    qkv_w, out_w, ctrl_w, gain_one, gain_two = (
        lax.all_gather(w_qkv, ("dp", "expert"), axis=0, tiled=True),
        lax.all_gather(w_out, ("dp", "expert"), axis=0, tiled=True),
        lax.all_gather(w_ctrl, ("dp", "expert"), axis=0, tiled=True),
        lax.all_gather(gain_attn, ("dp", "expert"), axis=0, tiled=True),
        lax.all_gather(gain_mix, ("dp", "expert"), axis=0, tiled=True),
    )
    tok_rows, feat_width = tokens.shape
    experts_all = ctrl_w.shape[1]
    group_rows = tok_rows // G
    length = seq_lengths[0]
    slot_order = group_map[0]
    token_slots = (
        jnp.zeros((tok_rows,), jnp.int32).at[slot_order].set(jnp.arange(tok_rows, dtype=jnp.int32))
    )
    source_one = tokens.astype(jnp.float32)
    scale_one = rms_scale(source_one)
    normed_one = (source_one * scale_one * gain_one.astype(jnp.float32)).astype(jnp.bfloat16)
    qkv_low = jnp.dot(normed_one, qkv_w, preferred_element_type=jnp.float32).astype(jnp.bfloat16)
    queries, key_rows, value_rows = split_parts(qkv_low, HEADS)
    attended, log_totals = attend_forward(queries, key_rows, value_rows, length)
    hidden = source_one + jnp.dot(attended, out_w, preferred_element_type=jnp.float32)
    scale_two = rms_scale(hidden)
    normed_two = (hidden * scale_two * gain_two.astype(jnp.float32)).astype(jnp.bfloat16)
    logits = jnp.dot(normed_two, ctrl_w, preferred_element_type=jnp.float32)
    slot_inputs = jnp.take(normed_two, slot_order, axis=0).reshape(group_rows, G, feat_width)
    slot_logits = jnp.take(logits, slot_order, axis=0).reshape(group_rows, G, experts_all)
    peak_logit = jnp.max(slot_logits, axis=1, keepdims=True)
    exp_logits = jnp.exp(slot_logits - peak_logit)
    weights = exp_logits / jnp.sum(exp_logits, axis=1, keepdims=True)
    weights_low = weights.astype(jnp.bfloat16)
    mixed = jnp.einsum(
        "gte,gtd->egd", weights_low, slot_inputs, preferred_element_type=jnp.float32
    ).astype(jnp.bfloat16)
    arrived = lax.all_to_all(mixed, "expert", split_axis=0, concat_axis=1, tiled=True)
    pre_act = jnp.einsum("erd,edf->erf", arrived, w_up, preferred_element_type=jnp.float32)
    activated = jax.nn.gelu(pre_act, approximate=False).astype(jnp.bfloat16)
    produced = jnp.einsum(
        "erf,efd->erd", activated, w_down, preferred_element_type=jnp.float32
    ).astype(jnp.bfloat16)
    returned = lax.all_to_all(produced, "expert", split_axis=1, concat_axis=0, tiled=True)
    combined = jnp.einsum(
        "gte,egd->gtd", weights_low, returned, preferred_element_type=jnp.float32
    ).reshape(tok_rows, feat_width)
    output = (hidden + jnp.take(combined, token_slots, axis=0)).astype(jnp.bfloat16)
    slot_grad = jnp.take(cotangent, slot_order, axis=0).reshape(group_rows, G, feat_width)
    grad_returned = jnp.einsum(
        "gte,gtd->egd", weights_low, slot_grad, preferred_element_type=jnp.float32
    ).astype(jnp.bfloat16)
    grad_weights = jnp.einsum(
        "gtd,egd->gte", slot_grad, returned, preferred_element_type=jnp.float32
    )
    grad_produced = lax.all_to_all(grad_returned, "expert", split_axis=0, concat_axis=1, tiled=True)
    grad_down = jnp.einsum(
        "erf,erd->efd", activated, grad_produced, preferred_element_type=jnp.float32
    )
    grad_act = jnp.einsum("erd,efd->erf", grad_produced, w_down, preferred_element_type=jnp.float32)
    grad_pre = (grad_act * gelu_slope(pre_act)).astype(jnp.bfloat16)
    grad_up = jnp.einsum("erd,erf->edf", arrived, grad_pre, preferred_element_type=jnp.float32)
    grad_arrived = jnp.einsum(
        "erf,edf->erd", grad_pre, w_up, preferred_element_type=jnp.float32
    ).astype(jnp.bfloat16)
    grad_mixed = lax.all_to_all(grad_arrived, "expert", split_axis=1, concat_axis=0, tiled=True)
    grad_up_shard, grad_down_shard = (
        lax.psum_scatter(
            grad_up.astype(jnp.bfloat16), "dp", scatter_dimension=1, tiled=True
        ).astype(jnp.float32),
        lax.psum_scatter(
            grad_down.astype(jnp.bfloat16), "dp", scatter_dimension=1, tiled=True
        ).astype(jnp.float32),
    )
    qkv_w, out_w, ctrl_w, gain_one, gain_two = (
        lax.all_gather(w_qkv, ("dp", "expert"), axis=0, tiled=True),
        lax.all_gather(w_out, ("dp", "expert"), axis=0, tiled=True),
        lax.all_gather(w_ctrl, ("dp", "expert"), axis=0, tiled=True),
        lax.all_gather(gain_attn, ("dp", "expert"), axis=0, tiled=True),
        lax.all_gather(gain_mix, ("dp", "expert"), axis=0, tiled=True),
    )
    grad_weights = grad_weights + jnp.einsum(
        "gtd,egd->gte", slot_inputs, grad_mixed, preferred_element_type=jnp.float32
    )
    grad_slot_inputs = jnp.einsum(
        "gte,egd->gtd", weights_low, grad_mixed, preferred_element_type=jnp.float32
    )
    grad_slot_logits = weights * (
        grad_weights - jnp.sum(weights * grad_weights, axis=1, keepdims=True)
    )
    grad_logits = jnp.take(
        grad_slot_logits.reshape(tok_rows, experts_all), token_slots, axis=0
    ).astype(jnp.bfloat16)
    grad_normed_two = jnp.take(grad_slot_inputs.reshape(tok_rows, feat_width), token_slots, axis=0)
    grad_normed_two = grad_normed_two + jnp.dot(
        grad_logits, ctrl_w.T, preferred_element_type=jnp.float32
    )
    grad_ctrl = jnp.dot(normed_two.T, grad_logits, preferred_element_type=jnp.float32)
    grad_gain_two, grad_from_norm = norm_backward(
        grad_normed_two, hidden, scale_two, gain_two.astype(jnp.float32)
    )
    grad_hidden = cotangent.astype(jnp.float32) + grad_from_norm
    grad_hidden_low = grad_hidden.astype(jnp.bfloat16)
    grad_out_w = jnp.dot(attended.T, grad_hidden_low, preferred_element_type=jnp.float32)
    grad_attended = jnp.dot(grad_hidden_low, out_w.T, preferred_element_type=jnp.float32).astype(
        jnp.bfloat16
    )
    grad_qkv = attend_backward(queries, key_rows, value_rows, log_totals, grad_attended, length)
    grad_qkv_w = jnp.dot(normed_one.T, grad_qkv, preferred_element_type=jnp.float32)
    grad_normed_one = jnp.dot(grad_qkv, qkv_w.T, preferred_element_type=jnp.float32)
    grad_gain_one, grad_from_first = norm_backward(
        grad_normed_one, source_one, scale_one, gain_one.astype(jnp.float32)
    )
    grad_tokens = (grad_hidden + grad_from_first).astype(jnp.bfloat16)
    shard_qkv, shard_out, shard_ctrl, shard_gain_one, shard_gain_two = (
        lax.psum_scatter(grad_qkv_w, ("dp", "expert"), scatter_dimension=0, tiled=True),
        lax.psum_scatter(grad_out_w, ("dp", "expert"), scatter_dimension=0, tiled=True),
        lax.psum_scatter(grad_ctrl, ("dp", "expert"), scatter_dimension=0, tiled=True),
        lax.psum_scatter(grad_gain_one, ("dp", "expert"), scatter_dimension=0, tiled=True),
        lax.psum_scatter(grad_gain_two, ("dp", "expert"), scatter_dimension=0, tiled=True),
    )
    return (
        output,
        grad_tokens,
        shard_gain_one,
        shard_gain_two,
        shard_qkv,
        shard_out,
        shard_ctrl,
        grad_up_shard,
        grad_down_shard,
    )


def solution(mesh):
    placed = (
        P(("dp", "expert"), None),
        P(("dp", "expert")),
        P(("dp", "expert"), None),
        P(("dp", "expert")),
        P(("dp", "expert")),
        P(("dp", "expert"), None),
        P(("dp", "expert"), None),
        P(("dp", "expert"), None),
        P("expert", None, None),
        P("expert", None, None),
        P(("dp", "expert"), None),
    )
    return jax.shard_map(
        on_device,
        mesh=mesh,
        in_specs=placed,
        out_specs=(
            P(("dp", "expert"), None),
            P(("dp", "expert"), None),
            P(("dp", "expert")),
            P(("dp", "expert")),
            P(("dp", "expert"), None),
            P(("dp", "expert"), None),
            P(("dp", "expert"), None),
            P("expert", "dp", None),
            P("expert", "dp", None),
        ),
        check_vma=False,
    )
```

profile of v0, /device:TPU:0, one launch (start us, length us, event | category | flops | bytes accessed | tf_op | source)
XLA Modules:
  0.0 1201.0 jit_solution(689461986090391828)
XLA Ops:
  10.3 42.0 %all-reduce.5 = (bf16[512]{0:T(512)(128)(2,1)S(1)}, bf16[512]{0:T(512)(128)(2,1)S(1)}) all-reduce(bf16[512]{0:T(512)(128)(2,1)S(1)} %dynamic-update-slice, bf16[512]{0:T(512)(128)(2,1)S(1)} %dynamic-update-slice.1), channel_id=1, replica_groups=mesh['dp'=8,'expert'=4] {'dp','expert'}, use_global_device_ids=true, to_apply=%add | all-reduce | flops 1024 | bytes 4096
  66.0 43.2 %all_gather.24 = bf16[512,16]{1,0:T(8,128)(2,1)} all-gather(bf16[16,16]{1,0:T(8,128)(2,1)S(1)} %copy-done.50), channel_id=1, replica_groups=mesh['dp'=8,'expert'=4] {'dp','expert'}, dimensions={0}, use_global_device_ids=true | all-gather | bytes 16896 | tf_op jit(solution)/shard_map/all_gather | solution.py:149
  112.5 40.7 %all_gather.22 = bf16[512,512]{1,0:T(8,128)(2,1)} all-gather(bf16[16,512]{1,0:T(8,128)(2,1)S(1)} %copy-done.46), channel_id=1, replica_groups=mesh['dp'=8,'expert'=4] {'dp','expert'}, dimensions={0}, use_global_device_ids=true | all-gather | bytes 540672 | tf_op jit(solution)/shard_map/all_gather | solution.py:148
  161.7 200.0 %while.33 = (s32[]{:T(128)}, bf16[4,512,8,64]{1,3,2,0:T(8,128)(2,1)}, f32[4,8,512]{2,1,0:T(8,128)}, s32[4]{0:T(128)S(1)}, s32[]{:T(128)}, /*index=5*/s32[]{:T(12...) while((s32[]{:T(128)}, ...), condition=%wide.region_4.5_spmd, body=%wide.region_1.4_spmd.sunk | while | flops 2251571712 | bytes 110256352 | solution.py:69
  180.7 15.0 %fusion.147 = f32[8,512]{1,0:T(8,128)S(1)} fusion(f32[8,512,2048]{2,1,0:T(8,128)} %get-tuple-element.596, f32[8,512]{1,0:T(8,128)S(1)} %get-tuple-element.597, pred[512,2048]{1,0:T(8,128)(4,1)S(1)} %fusion.145), kind=kLoop, calls=%fused_computation.11.clone.1 | loop fusion | flops 33550336 | bytes 34635776 | tf_op jit(solution)/shard_map/while/body/eval_jaxpr/reduce_sum | solution.py:62
  195.6 15.6 %fusion.148 = bf16[4,512,8,64]{1,3,2,0:T(8,128)(2,1)} fusion(bf16[4,512,8,64]{1,3,2,0:T(8,128)(2,1)} %get-tuple-element.628, s32[]{:T(128)S(6)} %copy.112, bf16[2048,8,64]{0,2,1:T(8,128)(2,1)} %get-tuple-element.648, f32[8,512,2048]{2,1,0:T(8,128)} %get-tuple-element.596, f32[8,512]{1,0:T(8,128)S(1)} %fusion.147, ...), kind=kOutput, calls=%fused_computation.17.clone.1 | convolution fusion | flops 1115947008 | bytes 37257220 | tf_op jit(solution)/shard_map/while/body/eval_jaxpr/hqk,khd->qhd/dot_general | solution.py:64
  230.6 15.0 %fusion.147 = f32[8,512]{1,0:T(8,128)S(1)} fusion(f32[8,512,2048]{2,1,0:T(8,128)} %get-tuple-element.596, f32[8,512]{1,0:T(8,128)S(1)} %get-tuple-element.597, pred[512,2048]{1,0:T(8,128)(4,1)S(1)} %fusion.145), kind=kLoop, calls=%fused_computation.11.clone.1 | loop fusion | flops 33550336 | bytes 34635776 | tf_op jit(solution)/shard_map/while/body/eval_jaxpr/reduce_sum | solution.py:62
  245.6 15.5 %fusion.148 = bf16[4,512,8,64]{1,3,2,0:T(8,128)(2,1)} fusion(bf16[4,512,8,64]{1,3,2,0:T(8,128)(2,1)} %get-tuple-element.628, s32[]{:T(128)S(6)} %copy.112, bf16[2048,8,64]{0,2,1:T(8,128)(2,1)} %get-tuple-element.648, f32[8,512,2048]{2,1,0:T(8,128)} %get-tuple-element.596, f32[8,512]{1,0:T(8,128)S(1)} %fusion.147, ...), kind=kOutput, calls=%fused_computation.17.clone.1 | convolution fusion | flops 1115947008 | bytes 37257220 | tf_op jit(solution)/shard_map/while/body/eval_jaxpr/hqk,khd->qhd/dot_general | solution.py:64
  280.5 15.0 %fusion.147 = f32[8,512]{1,0:T(8,128)S(1)} fusion(f32[8,512,2048]{2,1,0:T(8,128)} %get-tuple-element.596, f32[8,512]{1,0:T(8,128)S(1)} %get-tuple-element.597, pred[512,2048]{1,0:T(8,128)(4,1)S(1)} %fusion.145), kind=kLoop, calls=%fused_computation.11.clone.1 | loop fusion | flops 33550336 | bytes 34635776 | tf_op jit(solution)/shard_map/while/body/eval_jaxpr/reduce_sum | solution.py:62
  295.5 15.5 %fusion.148 = bf16[4,512,8,64]{1,3,2,0:T(8,128)(2,1)} fusion(bf16[4,512,8,64]{1,3,2,0:T(8,128)(2,1)} %get-tuple-element.628, s32[]{:T(128)S(6)} %copy.112, bf16[2048,8,64]{0,2,1:T(8,128)(2,1)} %get-tuple-element.648, f32[8,512,2048]{2,1,0:T(8,128)} %get-tuple-element.596, f32[8,512]{1,0:T(8,128)S(1)} %fusion.147, ...), kind=kOutput, calls=%fused_computation.17.clone.1 | convolution fusion | flops 1115947008 | bytes 37257220 | tf_op jit(solution)/shard_map/while/body/eval_jaxpr/hqk,khd->qhd/dot_general | solution.py:64
  330.4 15.0 %fusion.147 = f32[8,512]{1,0:T(8,128)S(1)} fusion(f32[8,512,2048]{2,1,0:T(8,128)} %get-tuple-element.596, f32[8,512]{1,0:T(8,128)S(1)} %get-tuple-element.597, pred[512,2048]{1,0:T(8,128)(4,1)S(1)} %fusion.145), kind=kLoop, calls=%fused_computation.11.clone.1 | loop fusion | flops 33550336 | bytes 34635776 | tf_op jit(solution)/shard_map/while/body/eval_jaxpr/reduce_sum | solution.py:62
  345.4 15.5 %fusion.148 = bf16[4,512,8,64]{1,3,2,0:T(8,128)(2,1)} fusion(bf16[4,512,8,64]{1,3,2,0:T(8,128)(2,1)} %get-tuple-element.628, s32[]{:T(128)S(6)} %copy.112, bf16[2048,8,64]{0,2,1:T(8,128)(2,1)} %get-tuple-element.648, f32[8,512,2048]{2,1,0:T(8,128)} %get-tuple-element.596, f32[8,512]{1,0:T(8,128)S(1)} %fusion.147, ...), kind=kOutput, calls=%fused_computation.17.clone.1 | convolution fusion | flops 1115947008 | bytes 37257220 | tf_op jit(solution)/shard_map/while/body/eval_jaxpr/hqk,khd->qhd/dot_general | solution.py:64
  453.7 18.8 %fusion.34 = bf16[4,256,2048]{2,1,0:T(8,128)(2,1)S(1)} fusion(f32[4,256,2048]{2,1,0:T(8,128)S(1)} %get-tuple-element.465, u8[256,2048]{1,0:T(8,128)(4,1)S(1)} %get-tuple-element.393, u8[256,2048]{1,0:T(8,128)(4,1)S(1)} %get-tuple-element.392), kind=kLoop, calls=%fused_computation.74 | loop fusion | flops 146800640 | bytes 13631488 | tf_op jit(solution)/shard_map/convert_element_type | solution.py:182
  632.3 447.4 %while.34 = (s32[]{:T(128)}, f32[2048,8,64]{0,2,1:T(8,128)}, f32[2048,8,64]{0,2,1:T(8,128)}, bf16[4,512,8,64]{1,3,2,0:T(8,128)(2,1)}, s32[4]{0:T(128)S(1)}, /*in...) while((s32[]{:T(128)}, f32[2048,8,64]{0,2,1:T(8,128)}, ...), condition=%wide.region_13.17_spmd.clone, body=%wide.region_11.16_spmd.clone.sunk | while | flops 5452874240 | bytes 347185472 | solution.py:109
  639.4 17.7 %fusion.158 = f32[8,512,2048]{2,1,0:T(8,128)} fusion(bf16[2048,8,64]{0,2,1:T(8,128)(2,1)} %get-tuple-element.698, bf16[2048,8,64]{0,2,1:T(8,128)(2,1)} %get-tuple-element.697, s32[]{:T(128)S(6)} %select_n.205), kind=kOutput, calls=%fused_computation.46.clone.1 | convolution fusion | flops 1073741824 | bytes 36175876 | tf_op jit(solution)/shard_map/while/body/eval_jaxpr/qhd,khd->hqk/dot_general | solution.py:90
  657.1 24.9 %multiply_reduce_fusion.6 = (f32[8,512]{1,0:T(8,128)S(1)}, f32[8,512,2048]{2,1,0:T(8,128)}) fusion(f32[8,512,2048]{2,1,0:T(8,128)} %fusion.158, f32[8,512]{1,0:T(8,128)S(1)} %dynamic-slice_bitcast_fusion.2, bf16[2048,8,64]{0,2,1:T(8,128)(2,1)S(1)} %get-tuple-element.695, bf16[2048,8,64]{0,2,1:T(8,128)(2,1)} %get-tuple-element.692, ...), kind=kOutput, calls=%fused_computation.34.clone.1 | convolution fusion | flops 1115680768 | bytes 70811648 | tf_op jit(solution)/shard_map/while/body/eval_jaxpr/qhd,khd->hqk/dot_general | solution.py:43
  682.0 28.0 %multiply_convert_fusion.3 = bf16[8,512,2048]{2,1,0:T(8,128)(2,1)} fusion(f32[8,512,2048]{2,1,0:T(8,128)} %get-tuple-element.612, f32[8,512,2048]{2,1,0:T(8,128)} %fusion.158, f32[8,512]{1,0:T(8,128)S(1)} %get-tuple-element.613), kind=kLoop, calls=%fused_computation.33.clone.1 | loop fusion | flops 25165824 | bytes 83902464 | tf_op jit(solution)/shard_map/while/body/eval_jaxpr/convert_element_type | solution.py:94
  710.0 16.3 %bitcast_add_fusion.5 = f32[2048,8,64]{0,2,1:T(8,128)} fusion(f32[2048,8,64]{0,2,1:T(8,128)} %get-tuple-element.672, f32[8,512,2048]{2,1,0:T(8,128)} %get-tuple-element.612, pred[]{:T(512)S(6)} %compare.3, bf16[2048,8,64]{0,2,1:T(8,128)(2,1)} %get-tuple-element.697, s32[]{:T(128)S(6)} %select_n.205), kind=kOutput, calls=%fused_computation.38.clone.1 | convolution fusion | flops 1084227584 | bytes 42467332 | tf_op jit(solution)/shard_map/while/body/eval_jaxpr/hqk,qhd->khd/dot_general | solution.py:87
  750.4 17.7 %fusion.158 = f32[8,512,2048]{2,1,0:T(8,128)} fusion(bf16[2048,8,64]{0,2,1:T(8,128)(2,1)} %get-tuple-element.698, bf16[2048,8,64]{0,2,1:T(8,128)(2,1)} %get-tuple-element.697, s32[]{:T(128)S(6)} %select_n.205), kind=kOutput, calls=%fused_computation.46.clone.1 | convolution fusion | flops 1073741824 | bytes 36175876 | tf_op jit(solution)/shard_map/while/body/eval_jaxpr/qhd,khd->hqk/dot_general | solution.py:90
  768.1 24.7 %multiply_reduce_fusion.6 = (f32[8,512]{1,0:T(8,128)S(1)}, f32[8,512,2048]{2,1,0:T(8,128)}) fusion(f32[8,512,2048]{2,1,0:T(8,128)} %fusion.158, f32[8,512]{1,0:T(8,128)S(1)} %dynamic-slice_bitcast_fusion.2, bf16[2048,8,64]{0,2,1:T(8,128)(2,1)S(1)} %get-tuple-element.695, bf16[2048,8,64]{0,2,1:T(8,128)(2,1)} %get-tuple-element.692, ...), kind=kOutput, calls=%fused_computation.34.clone.1 | convolution fusion | flops 1115680768 | bytes 70811648 | tf_op jit(solution)/shard_map/while/body/eval_jaxpr/qhd,khd->hqk/dot_general | solution.py:43
  792.8 27.6 %multiply_convert_fusion.3 = bf16[8,512,2048]{2,1,0:T(8,128)(2,1)} fusion(f32[8,512,2048]{2,1,0:T(8,128)} %get-tuple-element.612, f32[8,512,2048]{2,1,0:T(8,128)} %fusion.158, f32[8,512]{1,0:T(8,128)S(1)} %get-tuple-element.613), kind=kLoop, calls=%fused_computation.33.clone.1 | loop fusion | flops 25165824 | bytes 83902464 | tf_op jit(solution)/shard_map/while/body/eval_jaxpr/convert_element_type | solution.py:94
  820.4 17.1 %bitcast_add_fusion.5 = f32[2048,8,64]{0,2,1:T(8,128)} fusion(f32[2048,8,64]{0,2,1:T(8,128)} %get-tuple-element.672, f32[8,512,2048]{2,1,0:T(8,128)} %get-tuple-element.612, pred[]{:T(512)S(6)} %compare.3, bf16[2048,8,64]{0,2,1:T(8,128)(2,1)} %get-tuple-element.697, s32[]{:T(128)S(6)} %select_n.205), kind=kOutput, calls=%fused_computation.38.clone.1 | convolution fusion | flops 1084227584 | bytes 42467332 | tf_op jit(solution)/shard_map/while/body/eval_jaxpr/hqk,qhd->khd/dot_general | solution.py:87
  862.6 17.4 %fusion.158 = f32[8,512,2048]{2,1,0:T(8,128)} fusion(bf16[2048,8,64]{0,2,1:T(8,128)(2,1)} %get-tuple-element.698, bf16[2048,8,64]{0,2,1:T(8,128)(2,1)} %get-tuple-element.697, s32[]{:T(128)S(6)} %select_n.205), kind=kOutput, calls=%fused_computation.46.clone.1 | convolution fusion | flops 1073741824 | bytes 36175876 | tf_op jit(solution)/shard_map/while/body/eval_jaxpr/qhd,khd->hqk/dot_general | solution.py:90
  880.0 24.7 %multiply_reduce_fusion.6 = (f32[8,512]{1,0:T(8,128)S(1)}, f32[8,512,2048]{2,1,0:T(8,128)}) fusion(f32[8,512,2048]{2,1,0:T(8,128)} %fusion.158, f32[8,512]{1,0:T(8,128)S(1)} %dynamic-slice_bitcast_fusion.2, bf16[2048,8,64]{0,2,1:T(8,128)(2,1)S(1)} %get-tuple-element.695, bf16[2048,8,64]{0,2,1:T(8,128)(2,1)} %get-tuple-element.692, ...), kind=kOutput, calls=%fused_computation.34.clone.1 | convolution fusion | flops 1115680768 | bytes 70811648 | tf_op jit(solution)/shard_map/while/body/eval_jaxpr/qhd,khd->hqk/dot_general | solution.py:43
  904.7 27.6 %multiply_convert_fusion.3 = bf16[8,512,2048]{2,1,0:T(8,128)(2,1)} fusion(f32[8,512,2048]{2,1,0:T(8,128)} %get-tuple-element.612, f32[8,512,2048]{2,1,0:T(8,128)} %fusion.158, f32[8,512]{1,0:T(8,128)S(1)} %get-tuple-element.613), kind=kLoop, calls=%fused_computation.33.clone.1 | loop fusion | flops 25165824 | bytes 83902464 | tf_op jit(solution)/shard_map/while/body/eval_jaxpr/convert_element_type | solution.py:94
  932.3 17.1 %bitcast_add_fusion.5 = f32[2048,8,64]{0,2,1:T(8,128)} fusion(f32[2048,8,64]{0,2,1:T(8,128)} %get-tuple-element.672, f32[8,512,2048]{2,1,0:T(8,128)} %get-tuple-element.612, pred[]{:T(512)S(6)} %compare.3, bf16[2048,8,64]{0,2,1:T(8,128)(2,1)} %get-tuple-element.697, s32[]{:T(128)S(6)} %select_n.205), kind=kOutput, calls=%fused_computation.38.clone.1 | convolution fusion | flops 1084227584 | bytes 42467332 | tf_op jit(solution)/shard_map/while/body/eval_jaxpr/hqk,qhd->khd/dot_general | solution.py:87
  974.6 17.5 %fusion.158 = f32[8,512,2048]{2,1,0:T(8,128)} fusion(bf16[2048,8,64]{0,2,1:T(8,128)(2,1)} %get-tuple-element.698, bf16[2048,8,64]{0,2,1:T(8,128)(2,1)} %get-tuple-element.697, s32[]{:T(128)S(6)} %select_n.205), kind=kOutput, calls=%fused_computation.46.clone.1 | convolution fusion | flops 1073741824 | bytes 36175876 | tf_op jit(solution)/shard_map/while/body/eval_jaxpr/qhd,khd->hqk/dot_general | solution.py:90
  992.1 24.7 %multiply_reduce_fusion.6 = (f32[8,512]{1,0:T(8,128)S(1)}, f32[8,512,2048]{2,1,0:T(8,128)}) fusion(f32[8,512,2048]{2,1,0:T(8,128)} %fusion.158, f32[8,512]{1,0:T(8,128)S(1)} %dynamic-slice_bitcast_fusion.2, bf16[2048,8,64]{0,2,1:T(8,128)(2,1)S(1)} %get-tuple-element.695, bf16[2048,8,64]{0,2,1:T(8,128)(2,1)} %get-tuple-element.692, ...), kind=kOutput, calls=%fused_computation.34.clone.1 | convolution fusion | flops 1115680768 | bytes 70811648 | tf_op jit(solution)/shard_map/while/body/eval_jaxpr/qhd,khd->hqk/dot_general | solution.py:43
  1016.8 27.6 %multiply_convert_fusion.3 = bf16[8,512,2048]{2,1,0:T(8,128)(2,1)} fusion(f32[8,512,2048]{2,1,0:T(8,128)} %get-tuple-element.612, f32[8,512,2048]{2,1,0:T(8,128)} %fusion.158, f32[8,512]{1,0:T(8,128)S(1)} %get-tuple-element.613), kind=kLoop, calls=%fused_computation.33.clone.1 | loop fusion | flops 25165824 | bytes 83902464 | tf_op jit(solution)/shard_map/while/body/eval_jaxpr/convert_element_type | solution.py:94
  1044.3 17.0 %bitcast_add_fusion.5 = f32[2048,8,64]{0,2,1:T(8,128)} fusion(f32[2048,8,64]{0,2,1:T(8,128)} %get-tuple-element.672, f32[8,512,2048]{2,1,0:T(8,128)} %get-tuple-element.612, pred[]{:T(512)S(6)} %compare.3, bf16[2048,8,64]{0,2,1:T(8,128)(2,1)} %get-tuple-element.697, s32[]{:T(128)S(6)} %select_n.205), kind=kOutput, calls=%fused_computation.38.clone.1 | convolution fusion | flops 1084227584 | bytes 42467332 | tf_op jit(solution)/shard_map/while/body/eval_jaxpr/hqk,qhd->khd/dot_general | solution.py:87
  1106.2 36.9 %all-reduce.4 = (f32[512]{0:T(512)S(1)}, f32[512]{0:T(512)S(1)}) all-reduce(f32[512]{0:T(512)S(1)} %get-tuple-element.394, f32[512]{0:T(512)S(1)} %copy-done.49), channel_id=2, replica_groups=mesh['dp'=8,'expert'=4] {'dp','expert'}, use_global_device_ids=true, to_apply=%region_16.20.clone | all-reduce | flops 1024 | bytes 8192
  1160.0 33.9 %reduce-scatter.6.cloned.1.call-done = f32[16,1536]{1,0:T(8,128)} async-done(((f32[512,1536]{1,0:T(8,128)}), f32[16,1536]{1,0:T(8,128)}) %reduce-scatter.6.cloned.1.call-update) | async-done | bytes 98320 | tf_op jit(solution)/shard_map/reduce_scatter | solution.py:258
  (275 shorter events, 485.4 us)
Async XLA Ops:
  7.2 49.6 %copy-start.34 = (s32[1,2048]{1,0:T(1,128)S(1)}, s32[1,2048]{1,0:T(1,128)}, u32[]{:S(2)}) copy-start(s32[1,2048]{1,0:T(1,128)} %param.23) | copy-start | bytes 24580
  7.2 49.6 %copy-start.1 = (bf16[2048,512]{1,0:T(8,128)(2,1)S(1)}, bf16[2048,512]{1,0:T(8,128)(2,1)}, u32[]{:S(2)}) copy-start(bf16[2048,512]{1,0:T(8,128)(2,1)} %param.31) | copy-start | bytes 6291460
  7.2 146.0 %all-gather.2.cloned.1.call-start = ((), (), s32[]{:S(2)}) async-start(), calls=%async_computation.9 | async-start | bytes 1622016 | tf_op jit(solution)/shard_map/all_gather | solution.py:147
  52.3 100.8 %copy-start.47 = (f32[512]{0:T(512)}, f32[512]{0:T(512)S(1)}, u32[]{:S(2)}) copy-start(f32[512]{0:T(512)S(1)} %convert_element_type.110) | copy-start | bytes 6148
  56.8 9.2 copy-start.32
  56.8 9.2 copy-start.50
  56.8 55.6 %copy-start.46 = (bf16[16,512]{1,0:T(8,128)(2,1)S(1)}, bf16[16,512]{1,0:T(8,128)(2,1)}, u32[]{:S(2)}) copy-start(bf16[16,512]{1,0:T(8,128)(2,1)} %param.27) | copy-start | bytes 49156
  112.5 46.3 %copy-start.38 = (f32[2048]{0:T(1024)}, f32[2048]{0:T(1024)S(1)}, u32[]{:S(2)}) copy-start(f32[2048]{0:T(1024)S(1)} %get-tuple-element.458) | copy-start | bytes 24580
  387.5 13.4 %copy-start.28 = (f32[64,16]{1,0:T(8,128)}, f32[64,16]{1,0:T(8,128)S(1)}, u32[]{:S(2)}) copy-start(f32[64,16]{1,0:T(8,128)S(1)} %get-tuple-element.442) | copy-start | bytes 12292
  389.1 11.8 copy-start.16
  389.5 11.5 copy-start.30
  389.8 11.1 copy-start.44
  407.7 18.0 %all-to-all-start = ((bf16[16,64,512]{2,1,0:T(8,128)(2,1)}), bf16[16,64,512]{2,1,0:T(8,128)(2,1)S(1)}, u32[]{:S(2)}, u32[]{:S(2)}) async-start(bf16[16,64,512]{2,1,0:T(8,128)(2,1)} %copy.67), calls=%async_computation | async-start | bytes 2097152 | tf_op jit(solution)/shard_map/all_to_all | solution.py:180
  425.6 18.8 %all-to-all-start.2 = ((bf16[16,64,512]{2,1,0:T(8,128)(2,1)}), bf16[16,64,512]{2,1,0:T(8,128)(2,1)}, u32[]{:S(2)}, u32[]{:S(2)}) async-start(bf16[16,64,512]{2,1,0:T(8,128)(2,1)} %copy.73), calls=%async_computation.2 | async-start | bytes 2097152 | tf_op jit(solution)/shard_map/all_to_all | solution.py:198
  429.9 724.5 %reduce-scatter.14.cloned.1.call-start = ((), (), s32[]{:S(2)}) async-start(), calls=%async_computation.14 | async-start | bytes 9437184 | tf_op jit(solution)/shard_map/reduce_scatter | solution.py:213
  445.7 26.8 %copy-start.20 = (bf16[4,4,64,512]{3,2,0,1:T(8,128)(2,1)}, bf16[4,4,64,512]{3,2,0,1:T(8,128)(2,1)S(1)}, u32[]{:S(2)}) copy-start(bf16[4,4,64,512]{3,2,0,1:T(8,128)(2,1)S(1)} %copy.74) | copy-start | bytes 3145732
  453.7 18.8 %copy-start.18 = (f32[4,256,2048]{2,1,0:T(8,128)}, f32[4,256,2048]{2,1,0:T(8,128)S(1)}, u32[]{:S(2)}) copy-start(f32[4,256,2048]{2,1,0:T(8,128)S(1)} %get-tuple-element.465) | copy-start | bytes 25165828
  480.2 677.1 %reduce-scatter.12.cloned.1.call-start = ((), (), s32[]{:S(2)}) async-start(), calls=%async_computation.13 | async-start | bytes 9437184 | tf_op jit(solution)/shard_map/reduce_scatter | solution.py:210
  510.0 18.0 %all-to-all-start.3 = ((bf16[4,256,512]{2,0,1:T(4,128)(2,1)}), bf16[4,256,512]{2,0,1:T(4,128)(2,1)S(1)}, u32[]{:S(2)}, u32[]{:S(2)}) async-start(bf16[4,256,512]{2,0,1:T(4,128)(2,1)} %copy.75), calls=%async_computation.3 | async-start | bytes 2097152 | tf_op jit(solution)/shard_map/all_to_all | solution.py:208
  520.8 11.4 copy-start.35
  527.9 19.7 %all-to-all-start.1 = ((bf16[4,256,512]{2,0,1:T(4,128)(2,1)}), bf16[4,256,512]{2,0,1:T(4,128)(2,1)}, u32[]{:S(2)}, u32[]{:S(2)}) async-start(bf16[4,256,512]{2,0,1:T(4,128)(2,1)} %copy.69), calls=%async_computation.1 | async-start | bytes 2097152 | tf_op jit(solution)/shard_map/all_to_all | solution.py:186
  532.2 627.9 %reduce-scatter.10.cloned.1.call-start = ((), (), s32[]{:S(2)}) async-start(), calls=%async_computation.12 | async-start | bytes 270336 | tf_op jit(solution)/shard_map/reduce_scatter | solution.py:260
  607.5 8.0 copy-start.40
  615.5 9.6 copy-start.11
  627.4 532.6 %reduce-scatter.8.cloned.1.call-start = ((), (), s32[]{:S(2)}) async-start(), calls=%async_computation.11 | async-start | bytes 1081344 | tf_op jit(solution)/shard_map/reduce_scatter | solution.py:259
  632.3 561.7 %reduce-scatter.6.cloned.1.call-start = ((), (), s32[]{:S(2)}) async-start(), calls=%async_computation.10 | async-start | bytes 3244032 | tf_op jit(solution)/shard_map/reduce_scatter | solution.py:258
  726.4 10.9 copy-start
  837.4 10.8 copy-start
  949.4 10.8 copy-start
  1061.3 10.7 copy-start
  1098.2 8.0 copy-start.49
  1098.2 46.1 %copy-start.37 = (f32[2048]{0:T(1024)S(1)}, f32[2048]{0:T(1024)}, u32[]{:S(2)}) copy-start(f32[2048]{0:T(1024)} %get-tuple-element.457) | copy-start | bytes 24580
  (32 other events, 132.4 us)
Sparse Core Ops, SparseCore 0:
  10.9 57.6 all-gather.1
  480.3 145.5 reduce-scatter.13
  630.0 148.3 reduce-scatter.11
  781.0 132.4 reduce-scatter.9
  916.3 130.7 reduce-scatter.7
  1094.4 99.4 reduce-scatter.5
where the time goes:
time: 1210 us; the launch traced here: 1200 us
  matrix products  521 us (43%)
  other arithmetic  249 us (21%)
  blocking collectives  163 us (13%)
  local copies, waits for them, and re-layouts  158 us (13%)
  waiting for transfers between devices  64 us (5%)
  starting transfers between devices  15.8 us (1%)
  between operations  15.7 us (1%)
  loops' own time  14.6 us (1%)
    dot_general x8, matrix products, block_scores(): jnp.einsum('qhd,khd->hqk', query_block, key_rows, preferred_element_type=...  158 us
    convert_element_type x4, other arithmetic, one_block(): grad_scores = (probs * (grad_probs - row_total)).astype(jnp.bfloat16)  111 us
    unnamed x2, blocking collectives  78.9 us
    dot_general x4, matrix products, one_block(): jnp.einsum('qhd,khd->hqk', grad_block, value_rows, preferred_element_type...  70.3 us
    dot_general x4, matrix products, one_block(): jnp.einsum('hqk,qhd->khd', probs_low, grad_block, preferred_element_type=...  67.5 us
    dot_general x4, matrix products, one_block(): jnp.einsum('hqk,khd->qhd', probs_low, value_rows, preferred_element_type=...  62.2 us
    reduce_sum x4, other arithmetic, one_block(): total = jnp.sum(exp_scores, axis=-1, keepdims=True)  59.9 us
    all_gather x1, blocking collectives, on_device(): lax.all_gather(w_ctrl, ('dp', 'expert'), axis=0, tiled=True)  43.2 us
  transfers between devices with their start and end apart: 10, of which 4 were waited for; matrix products, arithmetic and copies ran while one was open for 52% of the time, Pallas kernels for 0%

commit v1 on v0

v1 whole, which is shorter than its diff:
```python
import functools

import jax
import jax.numpy as jnp
from jax import lax
from jax.experimental import pallas as pl
from jax.experimental.pallas import tpu as pltpu
from jax.sharding import PartitionSpec as P

HEADS = 8
G = 32
BQ = 256

eps_norm = 1e-05
masked_value = -1e30
bf16 = jnp.bfloat16
f32 = jnp.float32
NN = (((1,), (0,)), ((), ()))
NT = (((1,), (1,)), ((), ()))
TN = (((0,), (0,)), ((), ()))
VMEM_BYTES = 56 * 2**20


def dot(left, right, dims=NN):
    return lax.dot_general(left, right, dims, preferred_element_type=f32)


def rms_scale(values):
    return lax.rsqrt(jnp.mean(values * values, axis=-1, keepdims=True) + eps_norm)


def call(body, out_shape, args, cost, **extra):
    return pl.pallas_call(
        body,
        out_shape=out_shape,
        compiler_params=pltpu.CompilerParams(vmem_limit_bytes=VMEM_BYTES),
        cost_estimate=pl.CostEstimate(flops=cost[0], bytes_accessed=cost[1], transcendentals=cost[2]),
        **extra,
    )(*args)


def shape_of(dims, kind):
    return jax.ShapeDtypeStruct(dims, kind)


def prep_kernel(tok_ref, gmap_ref, unit_ref, gid_ref):
    rows = tok_ref.shape[0]
    step = 256
    for at in range(0, rows, step):
        block = tok_ref[at : at + step, :].astype(f32)
        unit_ref[at : at + step, :] = (block * rms_scale(block)).astype(bf16)
    groups = rows // G
    places = lax.broadcasted_iota(jnp.int32, (groups, rows), 1)
    group_at = lax.broadcasted_iota(jnp.int32, (groups, rows), 0)
    gmap = gmap_ref[...]
    member = jnp.zeros((groups, rows), jnp.int32)
    for slot in range(G):
        member = jnp.where(gmap[:, slot : slot + 1] == places, group_at, member)
    gid_ref[...] = jnp.sum(member.astype(f32), axis=0, keepdims=True).astype(jnp.int32)


def attend_kernel(len_ref, q_ref, k_ref, v_ref, out_ref, lse_ref, vt_ref):
    rows = q_ref.shape[0]
    lane = lax.broadcasted_iota(jnp.int32, (1, 128), 1) // 64
    vt_ref[...] = jnp.transpose(v_ref[...])

    def query_block(at, low):
        high = at + BQ
        queries = q_ref[at:high, :] * bf16(0.125)
        key_pos = lax.broadcasted_iota(jnp.int32, (BQ, BQ), 0)
        query_pos = lax.broadcasted_iota(jnp.int32, (BQ, BQ), 1)
        parts = []
        for head in range(2):
            own = jnp.where(lane == head, queries, bf16(0))
            near = jnp.where(key_pos <= query_pos, dot(k_ref[at:high, :], own, NT), masked_value)
            peak = jnp.max(near, axis=0, keepdims=True)
            if at > low:
                far = dot(k_ref[low:at, :], own, NT)
                peak = jnp.maximum(peak, jnp.max(far, axis=0, keepdims=True))
            near = jnp.exp(near - peak)
            total = jnp.sum(near, axis=0, keepdims=True)
            span = slice(64 * head, 64 * head + 64)
            mixed = dot(vt_ref[span, at:high], near.astype(bf16))
            if at > low:
                far = jnp.exp(far - peak)
                total = total + jnp.sum(far, axis=0, keepdims=True)
                mixed = mixed + dot(vt_ref[span, low:at], far.astype(bf16))
            parts.append(mixed * (1.0 / total))
            lse_ref[0, head : head + 1, at:high] = peak + jnp.log(total)
        out_ref[at:high, :] = jnp.transpose(jnp.concatenate(parts, 0)).astype(bf16)

    @pl.when(len_ref[0] == BQ)
    def _():
        for at in range(0, rows, BQ):
            query_block(at, at)

    @pl.when(len_ref[0] != BQ)
    def _():
        for at in range(0, rows, BQ):
            query_block(at, 0)


def attend_forward(qkv, length):
    rows, triple = qkv.shape
    width = triple // 3
    pairs = width // 128

    def part(offset):
        return pl.BlockSpec((rows, 128), lambda pair, _: (0, offset + pair))

    return call(
        attend_kernel,
        (shape_of((rows, width), bf16), shape_of((pairs, 2, rows), f32)),
        (length, qkv, qkv, qkv),
        (2 * rows * rows * width * 2, 8 * rows * width, rows * rows * HEADS // 2),
        grid_spec=pltpu.PrefetchScalarGridSpec(
            num_scalar_prefetch=1,
            grid=(pairs,),
            in_specs=[part(0), part(pairs), part(2 * pairs)],
            out_specs=[part(0), pl.BlockSpec((1, 2, rows), lambda pair, _: (pair, 0, 0))],
            scratch_shapes=[pltpu.VMEM((128, rows), bf16)],
        ),
    )


def attend_back_kernel(
    len_ref, q_ref, k_ref, v_ref, go_ref, o_ref, lse_ref, gq_ref, gk_ref, gv_ref, gqt_ref, kt_ref, dl_ref
):
    rows = q_ref.shape[0]
    step = 512
    lane = lax.broadcasted_iota(jnp.int32, (1, 128), 1) // 64
    kt_ref[...] = jnp.transpose(k_ref[...]) * bf16(0.125)
    product = jnp.transpose(go_ref[...].astype(f32) * o_ref[...].astype(f32))
    dl_ref[0:1, :] = jnp.sum(product[0:64], axis=0, keepdims=True)
    dl_ref[1:2, :] = jnp.sum(product[64:128], axis=0, keepdims=True)
    gqt_ref[...] = jnp.zeros_like(gqt_ref)

    def key_block(low, end):
        keys = k_ref[low : low + BQ, :] * bf16(0.125)
        vals = v_ref[low : low + BQ, :]
        grad_k = [None, None]
        grad_v = [None, None]
        spans = [(low, BQ)] + [(at, min(step, end - at)) for at in range(low + BQ, end, step)]
        for head in range(2):
            own_k = jnp.where(lane == head, keys, bf16(0))
            own_v = jnp.where(lane == head, vals, bf16(0))
            for at, wide in spans:
                here = slice(at, at + wide)
                probs = jnp.exp(dot(own_k, q_ref[here, :], NT) - lse_ref[0, head : head + 1, here])
                if at == low:
                    key_pos = lax.broadcasted_iota(jnp.int32, (BQ, BQ), 0)
                    query_pos = lax.broadcasted_iota(jnp.int32, (BQ, BQ), 1)
                    probs = jnp.where(key_pos <= query_pos, probs, 0.0)
                grad_probs = dot(own_v, go_ref[here, :], NT)
                grad_scores = (probs * (grad_probs - dl_ref[head : head + 1, here])).astype(bf16)
                more_v = dot(probs.astype(bf16), go_ref[here, :])
                more_k = dot(grad_scores, q_ref[here, :])
                grad_v[head] = more_v if grad_v[head] is None else grad_v[head] + more_v
                grad_k[head] = more_k if grad_k[head] is None else grad_k[head] + more_k
                span = slice(64 * head, 64 * head + 64)
                gqt_ref[span, here] += dot(kt_ref[span, low : low + BQ], grad_scores)
        gk_ref[low : low + BQ, :] = (jnp.where(lane == 0, grad_k[0], grad_k[1]) * 0.125).astype(bf16)
        gv_ref[low : low + BQ, :] = jnp.where(lane == 0, grad_v[0], grad_v[1]).astype(bf16)

    @pl.when(len_ref[0] == BQ)
    def _():
        for low in range(0, rows, BQ):
            key_block(low, low + BQ)

    @pl.when(len_ref[0] != BQ)
    def _():
        for low in range(0, rows, BQ):
            key_block(low, rows)

    gq_ref[...] = jnp.transpose(gqt_ref[...]).astype(bf16)


def attend_backward(qkv, attended, log_totals, grad_attended, length):
    rows, triple = qkv.shape
    width = triple // 3
    pairs = width // 128

    def part(offset):
        return pl.BlockSpec((rows, 128), lambda pair, _: (0, offset + pair))

    return call(
        attend_back_kernel,
        (shape_of((rows, width), bf16),) * 3,
        (length, qkv, qkv, qkv, grad_attended, attended, log_totals),
        (5 * rows * rows * width * 2, 16 * rows * width, rows * rows * HEADS // 2),
        grid_spec=pltpu.PrefetchScalarGridSpec(
            num_scalar_prefetch=1,
            grid=(pairs,),
            in_specs=[part(0), part(pairs), part(2 * pairs), part(0), part(0)]
            + [pl.BlockSpec((1, 2, rows), lambda pair, _: (pair, 0, 0))],
            out_specs=[part(0)] * 3,
            scratch_shapes=[pltpu.VMEM((128, rows), f32), pltpu.VMEM((128, rows), bf16), pltpu.VMEM((2, rows), f32)],
        ),
    )


def member_mask(gid_ref, groups, rows):
    return lax.broadcasted_iota(jnp.int32, (groups, rows), 0) == gid_ref[...]


def spread_weights(mask, wt_ref, w_ref):
    groups = mask.shape[0]
    for slot in range(wt_ref.shape[0]):
        wide = jnp.where(mask, wt_ref[slot : slot + 1, :], 0.0)
        w_ref[slot * groups : (slot + 1) * groups, :] = wide.astype(bf16)


def mix_kernel(
    tok_ref, att_ref, out_w_ref, gain_ref, ctrl_ref, gid_ref, cot_ref,
    hidden_ref, normed_ref, wt_ref, mixed_ref, grad_ref, w_ref,
):
    rows = tok_ref.shape[0]
    groups = rows // G
    step = 256
    for at in range(0, rows, step):
        here = slice(at, at + step)
        hidden = tok_ref[here, :].astype(f32) + dot(att_ref[here, :], out_w_ref[...])
        hidden_ref[here, :] = hidden
        normed_ref[here, :] = (hidden * rms_scale(hidden) * gain_ref[...]).astype(bf16)
    logits = dot(ctrl_ref[...], normed_ref[...], NT)
    mask = member_mask(gid_ref, groups, rows)
    for slot in range(logits.shape[0]):
        wide = jnp.where(mask, logits[slot : slot + 1, :], masked_value)
        wide = jnp.exp(wide - jnp.max(wide, axis=1, keepdims=True))
        wide = wide * (1.0 / jnp.sum(wide, axis=1, keepdims=True))
        wt_ref[slot : slot + 1, :] = jnp.sum(wide, axis=0, keepdims=True)
        w_ref[slot * groups : (slot + 1) * groups, :] = wide.astype(bf16)
    for at in range(0, w_ref.shape[0], step):
        here = slice(at, at + step)
        mixed_ref[here, :] = dot(w_ref[here, :], normed_ref[...]).astype(bf16)
        grad_ref[here, :] = dot(w_ref[here, :], cot_ref[...]).astype(bf16)


def combine_kernel(returned_ref, cot_ref, hidden_ref, wt_ref, gid_ref, out_ref, gw_ref, w_ref):
    rows = cot_ref.shape[0]
    groups = rows // G
    mask = member_mask(gid_ref, groups, rows)
    spread_weights(mask, wt_ref, w_ref)
    step = 256
    for at in range(0, rows, step):
        here = slice(at, at + step)
        combined = dot(w_ref[:, here], returned_ref[...], TN)
        out_ref[here, :] = (hidden_ref[here, :] + combined).astype(bf16)
    for slot in range(wt_ref.shape[0]):
        wide = dot(returned_ref[slot * groups : (slot + 1) * groups, :], cot_ref[...], NT)
        gw_ref[slot : slot + 1, :] = jnp.sum(jnp.where(mask, wide, 0.0), axis=0, keepdims=True)


def mix_back_kernel(
    gm_ref, cot_ref, normed_ref, hidden_ref, wt_ref, gw_ref, gid_ref, ctrl_ref, gain_ref, out_w_ref, att_ref,
    gh_ref, gatt_ref, gout_ref, gctrl_ref, w_ref, gl_ref, low_ref, gn_ref,
):
    rows, width = cot_ref.shape
    groups = rows // G
    experts = wt_ref.shape[0]
    mask = member_mask(gid_ref, groups, rows)
    spread_weights(mask, wt_ref, w_ref)
    for slot in range(experts):
        wide = dot(gm_ref[slot * groups : (slot + 1) * groups, :], normed_ref[...], NT)
        part = jnp.sum(jnp.where(mask, wide, 0.0), axis=0, keepdims=True) + gw_ref[slot : slot + 1, :]
        weight = wt_ref[slot : slot + 1, :]
        scaled = weight * part
        total = jnp.sum(jnp.where(mask, scaled, 0.0), axis=1, keepdims=True)
        back = jnp.sum(jnp.where(mask, total, 0.0), axis=0, keepdims=True)
        gl_ref[slot : slot + 1, :] = (scaled - weight * back).astype(bf16)
    gain = gain_ref[...]
    step = 256
    gain_total = jnp.zeros((1, width), f32)
    for at in range(0, rows, step):
        here = slice(at, at + step)
        grad_normed = dot(w_ref[:, here], gm_ref[...], TN) + dot(gl_ref[:, here], ctrl_ref[...], TN)
        hidden = hidden_ref[here, :]
        scale = rms_scale(hidden)
        unit = hidden * scale
        weighted = gain * grad_normed
        gain_total = gain_total + jnp.sum(grad_normed * unit, axis=0, keepdims=True)
        back = scale * (weighted - unit * jnp.mean(weighted * unit, axis=-1, keepdims=True))
        grad_hidden = cot_ref[here, :].astype(f32) + back
        gh_ref[here, :] = grad_hidden
        low = grad_hidden.astype(bf16)
        low_ref[here, :] = low
        gatt_ref[here, :] = dot(low, out_w_ref[...], NT).astype(bf16)
    gout_ref[...] = dot(att_ref[...], low_ref[...], TN).astype(bf16)
    small = [dot(gl_ref[...], normed_ref[...]), gain_total, jnp.zeros((127 - experts, width), f32)]
    gctrl_ref[...] = jnp.transpose(jnp.concatenate(small, 0)).astype(bf16)


def expert_kernel(pick_ref, in_ref, up_ref, down_ref, act_ref, slope_ref, out_ref, total_ref):
    step = 256
    first = pl.program_id(0) == 0
    last = pl.program_id(0) == pl.num_programs(0) - 1

    @pl.when(first)
    def _():
        total_ref[...] = jnp.zeros_like(total_ref)

    for at in range(0, in_ref.shape[0], step):
        here = slice(at, at + step)
        pre = dot(in_ref[here, :], up_ref[0])
        cdf = 0.5 + 0.5 * lax.erf(pre * 0.7071067811865476)
        density = jnp.exp(-0.5 * pre * pre) * 0.3989422804014327
        act = (pre * cdf).astype(bf16)
        act_ref[here, :] = act
        slope_ref[here, :] = (cdf + pre * density).astype(bf16)
        total_ref[here, :] += dot(act, down_ref[0])

    @pl.when(last)
    def _():
        out_ref[...] = total_ref[...].astype(bf16)


def expert_back_kernel(
    pick_ref, gp_ref, in_ref, act_ref, slope_ref, up_ref, down_ref, gup_ref, gdown_ref, out_ref, total_ref, pre_ref
):
    step = 256
    first = pl.program_id(0) == 0
    last = pl.program_id(0) == pl.num_programs(0) - 1

    @pl.when(first)
    def _():
        total_ref[...] = jnp.zeros_like(total_ref)

    gdown_ref[...] = dot(act_ref[...], gp_ref[...], TN).astype(bf16)
    for at in range(0, in_ref.shape[0], step):
        here = slice(at, at + step)
        grad_act = dot(gp_ref[here, :], down_ref[0], NT)
        grad_pre = (grad_act * slope_ref[here, :].astype(f32)).astype(bf16)
        pre_ref[here, :] = grad_pre
        total_ref[here, :] += dot(grad_pre, up_ref[0], NT)
    gup_ref[...] = dot(in_ref[...], pre_ref[...], TN).astype(bf16)

    @pl.when(last)
    def _():
        out_ref[...] = total_ref[...].astype(bf16)


def expert_specs(rows, width, hidden, step):
    whole = pl.BlockSpec((rows, width), lambda at, _: (0, 0))
    slab = pl.BlockSpec((rows, step), lambda at, _: (0, at))
    up = pl.BlockSpec((1, width, step), lambda at, pick: (pick[0], 0, at))
    down = pl.BlockSpec((1, step, width), lambda at, pick: (pick[0], at, 0))
    return whole, slab, up, down


def expert_forward(pick, arrived, w_up, w_down):
    rows, width = arrived.shape
    hidden = w_up.shape[2]
    step = 512
    whole, slab, up, down = expert_specs(rows, width, hidden, step)
    return call(
        expert_kernel,
        (shape_of((rows, hidden), bf16), shape_of((rows, hidden), bf16), shape_of((rows, width), bf16)),
        (pick, arrived, w_up, w_down),
        (4 * rows * width * hidden, 4 * rows * hidden + 4 * width * hidden + 4 * rows * width, 2 * rows * hidden),
        grid_spec=pltpu.PrefetchScalarGridSpec(
            num_scalar_prefetch=1,
            grid=(hidden // step,),
            in_specs=[whole, up, down],
            out_specs=[slab, slab, whole],
            scratch_shapes=[pltpu.VMEM((rows, width), f32)],
        ),
    )


def expert_backward(pick, grad_produced, arrived, act, slope, w_up, w_down):
    rows, width = arrived.shape
    hidden = w_up.shape[2]
    step = 512
    whole, slab, up, down = expert_specs(rows, width, hidden, step)
    return call(
        expert_back_kernel,
        (shape_of((width, hidden), bf16), shape_of((hidden, width), bf16), shape_of((rows, width), bf16)),
        (pick, grad_produced, arrived, act, slope, w_up, w_down),
        (8 * rows * width * hidden, 4 * rows * hidden + 8 * width * hidden + 6 * rows * width, 0),
        grid_spec=pltpu.PrefetchScalarGridSpec(
            num_scalar_prefetch=1,
            grid=(hidden // step,),
            in_specs=[whole, whole, slab, slab, up, down],
            out_specs=[
                pl.BlockSpec((width, step), lambda at, _: (0, at)),
                pl.BlockSpec((step, width), lambda at, _: (at, 0)),
                whole,
            ],
            scratch_shapes=[pltpu.VMEM((rows, width), f32), pltpu.VMEM((rows, step), bf16)],
        ),
    )


def project_kernel(unit_ref, w_ref, out_ref):
    out_ref[...] = dot(unit_ref[...], w_ref[...]).astype(bf16)


def project(unit, weights):
    rows, width = unit.shape
    wide = weights.shape[1]
    step = 512
    return call(
        project_kernel,
        shape_of((rows, wide), bf16),
        (unit, weights),
        (2 * rows * width * wide, 2 * (rows * width + rows * wide + width * wide), 0),
        grid=(rows // step,),
        in_specs=[pl.BlockSpec((step, width), lambda at: (at, 0)), pl.BlockSpec((width, wide), lambda at: (0, 0))],
        out_specs=pl.BlockSpec((step, wide), lambda at: (at, 0)),
    )


def weight_grad_kernel(unit_ref, gq_ref, gk_ref, gv_ref, out_ref):
    width = unit_ref.shape[1]
    for at, ref in enumerate((gq_ref, gk_ref, gv_ref)):
        out_ref[:, at * width : (at + 1) * width] = dot(unit_ref[...], ref[...], TN).astype(bf16)


def token_grad_kernel(gq_ref, gk_ref, gv_ref, w_ref, tok_ref, gh_ref, out_ref):
    width = tok_ref.shape[1]
    weighted = dot(gq_ref[...], w_ref[:, :width], NT)
    weighted = weighted + dot(gk_ref[...], w_ref[:, width : 2 * width], NT)
    weighted = weighted + dot(gv_ref[...], w_ref[:, 2 * width :], NT)
    source = tok_ref[...].astype(f32)
    scale = rms_scale(source)
    unit = source * scale
    back = scale * (weighted - unit * jnp.mean(weighted * unit, axis=-1, keepdims=True))
    out_ref[...] = (gh_ref[...] + back).astype(bf16)


def token_grad(grads, weights, tokens, grad_hidden):
    rows, width = tokens.shape
    step = 512
    block = pl.BlockSpec((step, width), lambda at: (at, 0))
    return call(
        token_grad_kernel,
        shape_of((rows, width), bf16),
        (*grads, weights, tokens, grad_hidden),
        (6 * rows * width * width, 14 * rows * width, 0),
        grid=(rows // step,),
        in_specs=[block] * 3 + [pl.BlockSpec(weights.shape, lambda at: (0, 0)), block, block],
        out_specs=block,
    )


def swap(array, axis, size, bit):
    return lax.ppermute(array, axis, [(at, at ^ bit) for at in range(size)])


def axis_bits(sizes):
    bits = []
    for axis, size in sizes:
        bit = size // 2
        while bit:
            bits.append((axis, size, bit))
            bit //= 2
    return bits


def gather_rows(shard, sizes):
    rows = shard.shape[0]
    total = rows
    for _, size in sizes:
        total *= size
    bits = axis_bits(sizes)
    held = shard[(None,) * len(bits)]
    for place in range(len(bits)):
        axis, size, bit = bits[place]
        other = swap(held, axis, size, bit)
        upper = (lax.axis_index(axis) // bit) % 2 == 1
        first = jnp.where(upper, other, held)
        second = jnp.where(upper, held, other)
        held = jnp.concatenate([first, second], axis=place)
    return held.reshape((total,) + shard.shape[1:])


def scatter_rows(whole, sizes, order):
    bits = axis_bits(sizes)
    devices = 2 ** len(bits)
    held = whole.reshape((2,) * len(bits) + (whole.shape[0] // devices,) + whole.shape[1:])
    left = list(range(len(bits)))
    for which in order:
        axis, size, bit = bits[which]
        place = left.index(which)
        mine = (lax.axis_index(axis) // bit) % 2
        keep = lax.dynamic_index_in_dim(held, mine, place, keepdims=False)
        send = lax.dynamic_index_in_dim(held, 1 - mine, place, keepdims=False)
        got = swap(send, axis, size, bit)
        held = keep.astype(f32) + got.astype(f32)
        left.pop(place)
        if left:
            held = held.astype(bf16)
    return held


def expert_grad_shard(grad, n_dp, per_owner):
    parts = n_dp // per_owner
    dp = lax.axis_index("dp")
    part, low = dp // per_owner, dp % per_owner
    rows = grad.shape[0] // parts
    total = lax.dynamic_slice_in_dim(grad, part * rows, rows, 0).astype(f32)
    for other in range(1, parts):
        away = lax.dynamic_slice_in_dim(grad, (part ^ other) * rows, rows, 0)
        total = total + swap(away, "dp", n_dp, other * per_owner).astype(f32)
    total = total.astype(bf16)
    rows //= per_owner
    groups = [[at * per_owner + own for own in range(per_owner)] for at in range(parts)]
    split = total.reshape((per_owner, rows) + grad.shape[1:])
    return lax.all_to_all(
        split, "dp", split_axis=0, concat_axis=0, axis_index_groups=groups, tiled=True
    ).astype(f32)


def on_device(
    n_dp, n_owner, tokens, seq_lengths, group_map, gain_attn, gain_mix, w_qkv, w_out, w_ctrl, w_up, w_down, cotangent
):
    rows, width = tokens.shape
    experts = w_ctrl.shape[1]
    per_owner = w_up.shape[0]
    groups = rows // G
    parts = n_dp // per_owner
    sizes = (("dp", n_dp), ("expert", n_owner))
    pick = (lax.axis_index("dp") % per_owner).astype(jnp.int32).reshape(1)

    gained = (w_qkv.astype(f32) * gain_attn.astype(f32)[:, None]).astype(bf16)
    qkv_w = gather_rows(gained, sizes)
    ctrl_slots = w_ctrl.reshape(-1, n_owner, per_owner).swapaxes(1, 2).reshape(-1, experts)
    pad = jnp.zeros((w_ctrl.shape[0], 127 - experts), bf16)
    late = gather_rows(jnp.concatenate([w_out, ctrl_slots, gain_mix[:, None], pad], 1), sizes)
    out_w = late[:, :width]
    small_t = late[:, width:].T
    ctrl_t = small_t[:experts]
    gain_two = small_t[experts : experts + 1].astype(f32)

    unit_one, gid = call(
        prep_kernel,
        (shape_of((rows, width), bf16), shape_of((1, rows), jnp.int32)),
        (tokens, group_map.reshape(groups, G)),
        (0, 4 * rows * width, 0),
    )
    qkv = project(unit_one, qkv_w)
    attended, log_totals = attend_forward(qkv, seq_lengths)

    slot_rows = experts * groups
    hidden, normed_two, weights, mixed, grad_returned = call(
        mix_kernel,
        (
            shape_of((rows, width), f32),
            shape_of((rows, width), bf16),
            shape_of((experts, rows), f32),
            shape_of((slot_rows, width), bf16),
            shape_of((slot_rows, width), bf16),
        ),
        (tokens, attended, out_w, gain_two, ctrl_t, gid, cotangent),
        (4 * slot_rows * rows * width + 2 * rows * width * width, 14 * rows * width, slot_rows * rows),
        scratch_shapes=[pltpu.VMEM((slot_rows, rows), bf16)],
    )

    teams = [
        [(part * per_owner + low) * n_owner + owner for low in range(per_owner) for owner in range(n_owner)]
        for part in range(parts)
    ]

    def exchange(array):
        split = array.reshape(experts, groups, width)
        moved = lax.all_to_all(
            split, ("dp", "expert"), split_axis=0, concat_axis=0, axis_index_groups=teams, tiled=True
        )
        return moved.reshape(slot_rows, width)

    arrived = exchange(mixed)
    grad_produced = exchange(grad_returned)
    act, slope, produced = expert_forward(pick, arrived, w_up, w_down)
    returned = exchange(produced)
    grad_up, grad_down, grad_arrived = expert_backward(pick, grad_produced, arrived, act, slope, w_up, w_down)
    grad_mixed = exchange(grad_arrived)
    grad_up_shard = expert_grad_shard(grad_up, n_dp, per_owner)
    grad_down_shard = expert_grad_shard(grad_down, n_dp, per_owner)

    output, grad_weights = call(
        combine_kernel,
        (shape_of((rows, width), bf16), shape_of((experts, rows), f32)),
        (returned, cotangent, hidden, weights, gid),
        (4 * slot_rows * rows * width, 10 * rows * width, 0),
        scratch_shapes=[pltpu.VMEM((slot_rows, rows), bf16)],
    )
    grad_hidden, grad_attended, grad_out, grad_small = call(
        mix_back_kernel,
        (
            shape_of((rows, width), f32),
            shape_of((rows, width), bf16),
            shape_of((width, width), bf16),
            shape_of((width, 128), bf16),
        ),
        (
            grad_mixed, cotangent, normed_two, hidden, weights, grad_weights, gid, ctrl_t, gain_two, out_w, attended
        ),
        (4 * slot_rows * rows * width + 4 * rows * width * width, 18 * rows * width, 0),
        scratch_shapes=[
            pltpu.VMEM((slot_rows, rows), bf16),
            pltpu.VMEM((experts, rows), bf16),
            pltpu.VMEM((rows, width), bf16),
            pltpu.VMEM((8, 128), f32),
        ],
    )
    order = list(range(len(axis_bits(sizes))))[::-1]
    early = scatter_rows(jnp.concatenate([grad_out, grad_small], 1), sizes, order)

    grads = attend_backward(qkv, attended, log_totals, grad_attended, seq_lengths)
    grad_w = call(
        weight_grad_kernel,
        shape_of((width, 3 * width), bf16),
        (unit_one, *grads),
        (6 * rows * width * width, 8 * rows * width, 0),
    )
    grad_tokens = token_grad(grads, qkv_w, tokens, grad_hidden)
    grad_w_shard = scatter_rows(grad_w, sizes, order)
    shard_qkv = gain_attn.astype(f32)[:, None] * grad_w_shard
    shard_gain_one = jnp.sum(w_qkv.astype(f32) * grad_w_shard, axis=1)
    shard_ctrl = early[:, width : width + experts]
    shard_ctrl = shard_ctrl.reshape(-1, per_owner, n_owner).swapaxes(1, 2).reshape(-1, experts)
    return (
        output,
        grad_tokens,
        shard_gain_one,
        early[:, width + experts],
        shard_qkv,
        early[:, :width],
        shard_ctrl,
        grad_up_shard,
        grad_down_shard,
    )


def solution(mesh):
    both = ("dp", "expert")
    rows = P(both, None)
    return jax.shard_map(
        functools.partial(on_device, mesh.shape["dp"], mesh.shape["expert"]),
        mesh=mesh,
        in_specs=(
            rows, P(both), rows, P(both), P(both), rows, rows, rows,
            P("expert", None, None), P("expert", None, None), rows,
        ),
        out_specs=(
            rows, rows, P(both), P(both), rows, rows, rows,
            P("expert", "dp", None), P("expert", "dp", None),
        ),
        check_vma=False,
    )
```

time: 1210 us -> 426 us (0.35)
  matrix products: 521 us -> 0 us
  other arithmetic: 249 us -> 18.2 us
  Pallas kernels: 0 us -> 222 us
  local copies, waits for them, and re-layouts: 158 us -> 12.3 us
  blocking collectives: 163 us -> 20.5 us
  waiting for transfers between devices: 64 us -> 97.4 us
  starting transfers between devices: 15.8 us -> 45.9 us
  loops' own time: 14.6 us -> 0 us
  between operations: 15.7 us -> 2.14 us
    dot_general x49 -> x0, matrix products: 521 us -> none  [the longest x8 158 us: block_scores(): jnp.einsum('qhd,khd->hqk', query_block, key_rows, preferred_element_type=...]
    pallas_call x0 -> x11, Pallas kernels: none -> 222 us  [call(): pl.pallas_call(body, out_shape=out_shape, compiler_params=pltpu.CompilerP...]
    convert_element_type x12 -> x14, other arithmetic: 144 us -> 9.59 us  [the longest x2 5.08 us: expert_grad_shard(): total = total.astype(bf16)]
    ppermute x0 -> x22, waiting for transfers between devices: none -> 92.7 us  [swap(): return lax.ppermute(array, axis, [(at, at ^ bit) for at in range(size)])]
    all_gather x2 -> x0, blocking collectives: 83.9 us -> none  [the longest x1 43.2 us: on_device(): lax.all_gather(w_ctrl, ('dp', 'expert'), axis=0, tiled=True)]
    unnamed x2 -> x0, blocking collectives: 78.9 us -> none
    gather x8 -> x0, local copies, waits for them, and re-layouts: 70.2 us -> none  [the longest x2 17.2 us: on_device(): jnp.take(combined, token_slots, axis=0)]
    reduce_sum x6 -> x0, other arithmetic: 62.3 us -> none  [the longest x4 59.9 us: one_block(): total = jnp.sum(exp_scores, axis=-1, keepdims=True)]
  transfers between devices with their start and end apart: 10 -> 27, of which waited for: 4 -> 13; matrix products, arithmetic and copies ran while one was open for 52% -> 6% of each run, Pallas kernels for 0% -> 37%
where the time goes in v1:
time: 426 us; the launch traced here: 418 us
  Pallas kernels  222 us (52%)
  waiting for transfers between devices  97.4 us (23%)
  starting transfers between devices  45.9 us (11%)
  blocking collectives  20.5 us (5%)
  other arithmetic  18.2 us (4%)
  local copies, waits for them, and re-layouts  12.3 us (3%)
    pallas_call x11, Pallas kernels, call(): pl.pallas_call(body, out_shape=out_shape, compiler_params=pltpu.CompilerP...  222 us
    ppermute x22, waiting for transfers between devices, swap(): return lax.ppermute(array, axis, [(at, at ^ bit) for at in range(size)])  92.7 us
    ppermute x22, starting transfers between devices, swap(): return lax.ppermute(array, axis, [(at, at ^ bit) for at in range(size)])  25.8 us
    all_to_all x1, blocking collectives, exchange(): lax.all_to_all(split, ('dp', 'expert'), split_axis=0, concat_axis=0, axis...  20.5 us
    all_to_all x3, starting transfers between devices, exchange(): lax.all_to_all(split, ('dp', 'expert'), split_axis=0, concat_axis=0, axis...  12.2 us
  transfers between devices with their start and end apart: 27, of which 13 were waited for; matrix products, arithmetic and copies ran while one was open for 6% of the time, Pallas kernels for 37%

profile of v1, /device:TPU:0, one launch (start us, length us, event | category | flops | bytes accessed | tf_op | source)
XLA Modules:
  0.0 418.4 jit_solution(13972342141733768253)
XLA Ops:
  3.1 4.0 collective-permute-start.5
  9.7 2.0 collective-permute-start.6
  11.7 2.2 collective-permute-done
  23.3 1.9 collective-permute-done.2
  29.4 5.9 %shard_map.178 = (bf16[2048,512]{1,0:T(8,128)(2,1)}, s32[1,2048]{1,0:T(1,128)}) custom-call(bf16[2048,512]{1,0:T(8,128)(2,1)} %tok_ref.5, s32[64,32]{1,0:T(8,128)} %reshape.100.gmap_ref), custom_call_target="tpu_custom_call" | custom-call | bytes 4194304 | tf_op jit(solution)/shard_map/pallas_call | solution.py:33
  41.1 7.4 %shard_map.179.q_ref.k_ref.v_ref = bf16[2048,1536]{1,0:T(8,128)(2,1)} custom-call(bf16[2048,512]{1,0:T(8,128)(2,1)} %get-tuple-element.33.unit_ref, bf16[512,1536]{1,0:T(8,128)(2,1)} %bitcast.91), custom_call_target="tpu_custom_call" | custom-call | flops 3221225472 | bytes 9961472 | tf_op jit(solution)/shard_map/pallas_call | solution.py:33
  48.4 49.7 %shard_map.180 = (bf16[2048,512]{1,0:T(8,128)(2,1)}, f32[4,2,2048]{2,1,0:T(2,128)}) custom-call(s32[1]{0:T(128)S(6)} %copy.104.len_ref, bf16[2048,1536]{1,0:T(8,128)(2,1)} %shard_map.179.q_ref.k_ref.v_ref, bf16[2048,1536]{1,0:T(8,128)(2,1)} %shard_map.179.q_ref.k_ref.v_ref, bf16[2048,1536]{1,0:T(8,128)(2,1)} %shard_map.179.q_ref.k_ref.v_ref), custom_call_target="tpu_custom_call" | custom-call | flops 8589934592 | bytes 8388608 | tf_op jit(solution)/shard_map/pallas_call | solution.py:33
  98.1 12.1 %shard_map.181 = (f32[2048,512]{1,0:T(8,128)}, bf16[2048,512]{1,0:T(8,128)(2,1)}, f32[16,2048]{1,0:T(8,128)}, bf16[1024,512]{1,0:T(8,128)(2,1)}, bf16[1024,512]{1,0:T(8,128)(2,1)}) custom-call(bf16[2048,512]{1,0:T(8,128)(2,1)} %tok_ref.5, bf16[2048,512]{1,0:T(8,128)(2,1)} %get-tuple-element.34.att_ref.o_ref, bf16[512,512]{1,0:T(8,128)(2,1)} %slice.28.out_w_ref, ...), custom_call_target="tpu_custom_call" | custom-call | flops 5368709120 | bytes 14680064 | tf_op jit(solution)/shard_map/pallas_call | solution.py:33
  110.2 20.5 %all_to_all.30 = bf16[16,64,512]{2,1,0:T(8,128)(2,1)} all-to-all(bf16[16,64,512]{2,1,0:T(8,128)(2,1)} %bitcast.104), channel_id=1, replica_groups={{0,1,2,3,4,5,6,7,8,9,10,11,12,13,14,15},{16,17,18,19,20,21,22,23,24,25,..., dimensions={0} | all-to-all | bytes 2097152 | tf_op jit(solution)/shard_map/all_to_all | solution.py:566
  130.8 3.7 all-to-all-start.2
  134.4 11.8 %shard_map.182 = (bf16[1024,2048]{1,0:T(8,128)(2,1)}, bf16[1024,2048]{1,0:T(8,128)(2,1)}, bf16[1024,512]{1,0:T(8,128)(2,1)}) custom-call(s32[1]{0:T(128)} %bitcast.pick_ref, bf16[1024,512]{1,0:T(8,128)(2,1)} %bitcast.93, bf16[4,512,2048]{2,1,0:T(8,128)(2,1)} %up_ref.3, bf16[4,2048,512]{2,1,0:T(8,128)(2,1)} %down_ref.3), custom_call_target="tpu_custom_call" | custom-call | flops 4294967296 | bytes 14680064 | tf_op jit(solution)/shard_map/pallas_call | solution.py:33
  146.3 4.3 %all-to-all-done.2 = bf16[16,64,512]{2,1,0:T(8,128)(2,1)S(1)} async-done(((bf16[16,64,512]{2,1,0:T(8,128)(2,1)}), bf16[16,64,512]{2,1,0:T(8,128)(2,1)S(1)}, u32[]{:S(2)}, u32[]{:S(2)}) %all-to-all-start.2) | async-done | bytes 1048608 | tf_op jit(solution)/shard_map/all_to_all | solution.py:566
  150.5 3.7 all-to-all-start.1
  154.2 15.8 %shard_map.184 = (bf16[512,2048]{1,0:T(8,128)(2,1)}, bf16[2048,512]{1,0:T(8,128)(2,1)}, bf16[1024,512]{1,0:T(8,128)(2,1)}) custom-call(s32[1]{0:T(128)} %bitcast.pick_ref, bf16[1024,512]{1,0:T(8,128)(2,1)} %bitcast.102, bf16[1024,512]{1,0:T(8,128)(2,1)} %bitcast.94, bf16[1024,2048]{1,0:T(8,128)(2,1)} %get-tuple-element.42.act_ref, ...), custom_call_target="tpu_custom_call" | custom-call | flops 8589934592 | bytes 19922944 | tf_op jit(solution)/shard_map/pallas_call | solution.py:33
  171.3 4.9 %all-to-all-start.3 = ((bf16[16,64,512]{2,1,0:T(8,128)(2,1)}), bf16[16,64,512]{2,1,0:T(8,128)(2,1)}, u32[]{:S(2)}, u32[]{:S(2)}) async-start(bf16[16,64,512]{2,1,0:T(8,128)(2,1)} %bitcast.101), calls=%async_computation.3 | async-start | bytes 2097152 | tf_op jit(solution)/shard_map/all_to_all | solution.py:566
  178.8 2.8 collective-permute-start.20
  181.6 68.0 %collective-permute-done.21 = bf16[1024,512]{1,0:T(8,128)(2,1)} collective-permute-done((bf16[1024,512]{1,0:T(8,128)(2,1)S(1)}, bf16[1024,512]{1,0:T(8,128)(2,1)}, u32[]{:S(2)}, u32[]{:S(2)}) %collective-permute-start.21) | collective-permute-done | bytes 1048608 | tf_op jit(solution)/shard_map/ppermute | solution.py:447
  249.6 2.5 add_convert_fusion
  252.1 16.2 %shard_map.183 = (bf16[2048,512]{1,0:T(8,128)(2,1)}, f32[16,2048]{1,0:T(8,128)}) custom-call(bf16[1024,512]{1,0:T(8,128)(2,1)} %bitcast.100, bf16[2048,512]{1,0:T(8,128)(2,1)} %cot_ref.5, f32[2048,512]{1,0:T(8,128)} %get-tuple-element.38.hidden_ref, f32[16,2048]{1,0:T(8,128)} %get-tuple-element.39.wt_ref, s32[1,2048]{1,0:T(1,128)} %get-tuple-element.35.gid_ref), custom_call_target="tpu_custom_call" | custom-call | flops 4294967296 | bytes 10485760 | tf_op jit(solution)/shard_map/pallas_call | solution.py:33
  268.3 4.0 all-to-all-start.5
  272.3 23.9 %shard_map.185 = (f32[2048,512]{1,0:T(8,128)}, bf16[2048,512]{1,0:T(8,128)(2,1)}, bf16[512,512]{1,0:T(8,128)(2,1)}, bf16[512,128]{1,0:T(8,128)(2,1)}) custom-call(bf16[1024,512]{1,0:T(8,128)(2,1)} %bitcast.17.gm_ref, bf16[2048,512]{1,0:T(8,128)(2,1)} %cot_ref.5, bf16[2048,512]{1,0:T(8,128)(2,1)} %get-tuple-element.45.normed_ref, ...), custom_call_target="tpu_custom_call" | custom-call | flops 6442450944 | bytes 18874368 | tf_op jit(solution)/shard_map/pallas_call | solution.py:33
  297.5 61.8 %shard_map.186 = (bf16[2048,512]{1,0:T(8,128)(2,1)}, bf16[2048,512]{1,0:T(8,128)(2,1)}, bf16[2048,512]{1,0:T(8,128)(2,1)}) custom-call(s32[1]{0:T(128)S(6)} %copy.104.len_ref, bf16[2048,1536]{1,0:T(8,128)(2,1)} %shard_map.179.q_ref.k_ref.v_ref, bf16[2048,1536]{1,0:T(8,128)(2,1)} %shard_map.179.q_ref.k_ref.v_ref, ...), custom_call_target="tpu_custom_call" | custom-call | flops 21474836480 | bytes 16777216 | tf_op jit(solution)/shard_map/pallas_call | solution.py:33
  359.3 8.0 %shard_map.188 = bf16[512,1536]{1,0:T(8,128)(2,1)} custom-call(bf16[2048,512]{1,0:T(8,128)(2,1)} %get-tuple-element.33.unit_ref, bf16[2048,512]{1,0:T(8,128)(2,1)} %get-tuple-element.49.gq_ref, bf16[2048,512]{1,0:T(8,128)(2,1)} %get-tuple-element.50.gk_ref, bf16[2048,512]{1,0:T(8,128)(2,1)} %get-tuple-element.51.gv_ref), custom_call_target="tpu_custom_call" | custom-call | flops 3221225472 | bytes 8388608 | tf_op jit(solution)/shard_map/pallas_call | solution.py:33
  369.2 2.6 add_convert_fusion.1
  371.8 4.0 collective-permute-done.16
  376.6 9.3 %shard_map.187 = bf16[2048,512]{1,0:T(8,128)(2,1)} custom-call(bf16[2048,512]{1,0:T(8,128)(2,1)} %get-tuple-element.49.gq_ref, bf16[2048,512]{1,0:T(8,128)(2,1)} %get-tuple-element.50.gk_ref, bf16[2048,512]{1,0:T(8,128)(2,1)} %get-tuple-element.51.gv_ref, bf16[512,1536]{1,0:T(8,128)(2,1)} %bitcast.92, bf16[2048,512]{1,0:T(8,128)(2,1)} %tok_ref.5, ...), custom_call_target="tpu_custom_call" | custom-call | flops 3221225472 | bytes 14680064 | tf_op jit(solution)/shard_map/pallas_call | solution.py:33
  387.2 1.8 collective-permute-start.12
  390.1 2.5 collective-permute-start.19
  392.6 3.9 all-to-all-start.4
  396.6 2.1 collective-permute-start.13
  398.7 11.4 %collective-permute-done.13 = bf16[2,16,1536]{2,1,0:T(8,128)(2,1)S(1)} collective-permute-done((bf16[2,16,1536]{2,1,0:T(8,128)(2,1)S(1)}, bf16[2,16,1536]{2,1,0:T(8,128)(2,1)S(1)}, u32[]{:S(2)}, u32[]{:S(2)}) %collective-permute-start.13) | collective-permute-done | bytes 98336 | tf_op jit(solution)/shard_map/ppermute | solution.py:447
  413.7 1.6 convert_element_type.201
  (117 shorter events, 40.0 us)
Async XLA Ops:
  3.1 5.8 %collective-permute-start.5 = (bf16[1,1,1,1,1,16,640]{6,5,4,3,2,1,0:T(8,128)(2,1)S(1)}, bf16[1,1,1,1,1,16,640]{6,5,4,3,2,1,0:T(8,128)(2,1)S(1)}, u32[]{:S(2)}, u32[]{:S(2)}) collective-permute-start(bf16[1,1,1,1,1,16,640]{6,5,4,3,2,1,0:T(8,128)(2,1)S(1)} %maximum_bitcast_fusion), channel_id=1, source_target_pairs={{0,16},{4,20},{8,24},{12,28},{16,0},{20,4},{24,8},{28,12},{1,17},{... | collective-permute-start | bytes 61448 | tf_op jit(solution)/shard_map/ppermute | solution.py:447
  7.8 19.6 %copy-start.5 = (s32[1,2048]{1,0:T(1,128)S(1)}, s32[1,2048]{1,0:T(1,128)}, u32[]{:S(2)}) copy-start(s32[1,2048]{1,0:T(1,128)} %param.13) | copy-start | bytes 24580
  8.7 5.2 %collective-permute-start = (bf16[1,1,1,1,1,16,1536]{6,5,4,3,2,1,0:T(8,128)(2,1)S(1)}, bf16[1,1,1,1,1,16,1536]{6,5,4,3,2,1,0:T(8,128)(2,1)S(1)}, u32[]{:S(2)}, u32[]{:S(2)}) collective-permute-start(bf16[1,1,1,1,1,16,1536]{6,5,4,3,2,1,0:T(8,128)(2,1)S(1)} %fusion.11), channel_id=1, source_target_pairs={{0,16},{4,20},{8,24},{12,28},{16,0},{20,4},{24,8},{28,12},{1,17},{... | collective-permute-start | bytes 147464 | tf_op jit(solution)/shard_map/ppermute | solution.py:447
  9.7 6.6 %collective-permute-start.6 = (bf16[2,1,1,1,1,16,640]{6,5,4,3,2,1,0:T(8,128)(2,1)S(1)}, bf16[2,1,1,1,1,16,640]{6,5,4,3,2,1,0:T(8,128)(2,1)S(1)}, u32[]{:S(2)}, u32[]{:S(2)}) collective-permute-start(bf16[2,1,1,1,1,16,640]{6,5,4,3,2,1,0:T(8,128)(2,1)S(1)} %pad_maximum_fusion.10), channel_id=1, source_target_pairs={{0,8},{4,12},{8,0},{12,4},{16,24},{20,28},{24,16},{28,20},{1,9},{5... | collective-permute-start | bytes 122888 | tf_op jit(solution)/shard_map/ppermute | solution.py:447
  14.8 4.7 %collective-permute-start.1 = (bf16[2,1,1,1,1,16,1536]{6,5,4,3,2,1,0:T(8,128)(2,1)S(1)}, bf16[2,1,1,1,1,16,1536]{6,5,4,3,2,1,0:T(8,128)(2,1)S(1)}, u32[]{:S(2)}, u32[]{:S(2)}) collective-permute-start(bf16[2,1,1,1,1,16,1536]{6,5,4,3,2,1,0:T(8,128)(2,1)S(1)} %pad_maximum_fusion.8), channel_id=1, source_target_pairs={{0,8},{4,12},{8,0},{12,4},{16,24},{20,28},{24,16},{28,20},{1,9},{5... | collective-permute-start | bytes 294920 | tf_op jit(solution)/shard_map/ppermute | solution.py:447
  16.4 5.3 %collective-permute-start.7 = (bf16[2,2,1,1,1,16,640]{6,5,4,3,2,1,0:T(8,128)(2,1)S(1)}, bf16[2,2,1,1,1,16,640]{6,5,4,3,2,1,0:T(8,128)(2,1)S(1)}, u32[]{:S(2)}, u32[]{:S(2)}) collective-permute-start(bf16[2,2,1,1,1,16,640]{6,5,4,3,2,1,0:T(8,128)(2,1)S(1)} %pad_maximum_fusion.9), channel_id=1, source_target_pairs={{0,4},{4,0},{8,12},{12,8},{16,20},{20,16},{24,28},{28,24},{1,5},{5... | collective-permute-start | bytes 245768 | tf_op jit(solution)/shard_map/ppermute | solution.py:447
  19.5 5.7 %collective-permute-start.2 = (bf16[2,2,1,1,1,16,1536]{6,5,4,3,2,1,0:T(8,128)(2,1)S(1)}, bf16[2,2,1,1,1,16,1536]{6,5,4,3,2,1,0:T(8,128)(2,1)S(1)}, u32[]{:S(2)}, u32[]{:S(2)}) collective-permute-start(bf16[2,2,1,1,1,16,1536]{6,5,4,3,2,1,0:T(8,128)(2,1)S(1)} %pad_maximum_fusion.6), channel_id=1, source_target_pairs={{0,4},{4,0},{8,12},{12,8},{16,20},{20,16},{24,28},{28,24},{1,5},{5... | collective-permute-start | bytes 589832 | tf_op jit(solution)/shard_map/ppermute | solution.py:447
  21.8 13.5 %collective-permute-start.8 = (bf16[2,2,2,1,1,16,640]{6,5,4,3,2,1,0:T(8,128)(2,1)S(1)}, bf16[2,2,2,1,1,16,640]{6,5,4,3,2,1,0:T(8,128)(2,1)S(1)}, u32[]{:S(2)}, u32[]{:S(2)}) collective-permute-start(bf16[2,2,2,1,1,16,640]{6,5,4,3,2,1,0:T(8,128)(2,1)S(1)} %pad_maximum_fusion.7), channel_id=1, source_target_pairs={{0,2},{1,3},{2,0},{3,1},{4,6},{5,7},{6,4},{7,5},{8,10},{9,11},{10,... | collective-permute-start | bytes 491528 | tf_op jit(solution)/shard_map/ppermute | solution.py:447
  25.4 10.1 %collective-permute-start.3 = (bf16[2,2,2,1,1,16,1536]{6,5,4,3,2,1,0:T(8,128)(2,1)S(1)}, bf16[2,2,2,1,1,16,1536]{6,5,4,3,2,1,0:T(8,128)(2,1)S(1)}, u32[]{:S(2)}, u32[]{:S(2)}) collective-permute-start(bf16[2,2,2,1,1,16,1536]{6,5,4,3,2,1,0:T(8,128)(2,1)S(1)} %pad_maximum_fusion.4), channel_id=1, source_target_pairs={{0,2},{1,3},{2,0},{3,1},{4,6},{5,7},{6,4},{7,5},{8,10},{9,11},{10,... | collective-permute-start | bytes 1179656 | tf_op jit(solution)/shard_map/ppermute | solution.py:447
  35.4 1.7 collective-permute-start.9
  35.6 4.0 collective-permute-start.4
  130.8 19.8 %all-to-all-start.2 = ((bf16[16,64,512]{2,1,0:T(8,128)(2,1)}), bf16[16,64,512]{2,1,0:T(8,128)(2,1)S(1)}, u32[]{:S(2)}, u32[]{:S(2)}) async-start(bf16[16,64,512]{2,1,0:T(8,128)(2,1)} %bitcast.14), calls=%async_computation.2 | async-start | bytes 2097152 | tf_op jit(solution)/shard_map/all_to_all | solution.py:566
  150.5 3.7 copy-start.3
  150.5 19.8 %all-to-all-start.1 = ((bf16[16,64,512]{2,1,0:T(8,128)(2,1)}), bf16[16,64,512]{2,1,0:T(8,128)(2,1)S(1)}, u32[]{:S(2)}, u32[]{:S(2)}) async-start(bf16[16,64,512]{2,1,0:T(8,128)(2,1)} %bitcast.103), calls=%async_computation.1 | async-start | bytes 2097152 | tf_op jit(solution)/shard_map/all_to_all | solution.py:566
  171.3 6.4 %copy-start = (bf16[512,2048]{1,0:T(8,128)(2,1)S(1)}, bf16[512,2048]{1,0:T(8,128)(2,1)}, u32[]{:S(2)}) copy-start(bf16[512,2048]{1,0:T(8,128)(2,1)} %get-tuple-element.55) | copy-start | bytes 6291460
  171.3 97.0 %all-to-all-start.3 = ((bf16[16,64,512]{2,1,0:T(8,128)(2,1)}), bf16[16,64,512]{2,1,0:T(8,128)(2,1)}, u32[]{:S(2)}, u32[]{:S(2)}) async-start(bf16[16,64,512]{2,1,0:T(8,128)(2,1)} %bitcast.101), calls=%async_computation.3 | async-start | bytes 2097152 | tf_op jit(solution)/shard_map/all_to_all | solution.py:566
  177.6 72.0 %collective-permute-start.21 = (bf16[1024,512]{1,0:T(8,128)(2,1)S(1)}, bf16[1024,512]{1,0:T(8,128)(2,1)}, u32[]{:S(2)}, u32[]{:S(2)}) collective-permute-start(bf16[1024,512]{1,0:T(8,128)(2,1)S(1)} %constant_dynamic-slice_fusion), channel_id=1, source_target_pairs={{0,16},{4,20},{8,24},{12,28},{16,0},{20,4},{24,8},{28,12},{1,17},{... | collective-permute-start | bytes 3145736 | tf_op jit(solution)/shard_map/ppermute | solution.py:447
  177.7 71.9 %copy-start.1 = (bf16[2048,512]{1,0:T(8,128)(2,1)S(1)}, bf16[2048,512]{1,0:T(8,128)(2,1)}, u32[]{:S(2)}) copy-start(bf16[2048,512]{1,0:T(8,128)(2,1)} %get-tuple-element.56) | copy-start | bytes 6291460
  178.8 190.4 %collective-permute-start.20 = (bf16[256,2048]{1,0:T(8,128)(2,1)}, bf16[256,2048]{1,0:T(8,128)(2,1)}, u32[]{:S(2)}, u32[]{:S(2)}) collective-permute-start(bf16[256,2048]{1,0:T(8,128)(2,1)} %constant_dynamic-slice_fusion.1), channel_id=1, source_target_pairs={{0,16},{4,20},{8,24},{12,28},{16,0},{20,4},{24,8},{28,12},{1,17},{... | collective-permute-start | bytes 3145736 | tf_op jit(solution)/shard_map/ppermute | solution.py:447
  268.3 124.3 %all-to-all-start.5 = ((bf16[4,256,512]{2,1,0:T(8,128)(2,1)}), bf16[4,256,512]{2,1,0:T(8,128)(2,1)S(1)}, u32[]{:S(2)}, u32[]{:S(2)}) async-start(bf16[4,256,512]{2,1,0:T(8,128)(2,1)} %bitcast.44), calls=%async_computation.5 | async-start | bytes 2097152 | tf_op jit(solution)/shard_map/all_to_all | solution.py:509
  297.4 71.6 %collective-permute-start.15 = (bf16[2,2,2,2,16,640]{5,4,3,2,1,0:T(8,128)(2,1)S(1)}, bf16[2,2,2,2,16,640]{5,4,3,2,1,0:T(8,128)(2,1)S(1)}, u32[]{:S(2)}, u32[]{:S(2)}) collective-permute-start(bf16[2,2,2,2,16,640]{5,4,3,2,1,0:T(8,128)(2,1)S(1)} %get-tuple-element.99), channel_id=1, source_target_pairs={{0,1},{1,0},{2,3},{3,2},{4,5},{5,4},{6,7},{7,6},{8,9},{9,8},{10,11... | collective-permute-start | bytes 983048 | tf_op jit(solution)/shard_map/ppermute | solution.py:447
  368.9 7.0 %collective-permute-start.10 = (bf16[2,2,2,2,16,1536]{5,4,0,1,2,3:T(8,128)(2,1)S(1)}, bf16[2,2,2,2,16,1536]{5,4,0,1,2,3:T(8,128)(2,1)S(1)}, u32[]{:S(2)}, u32[]{:S(2)}) collective-permute-start(bf16[2,2,2,2,16,1536]{5,4,0,1,2,3:T(8,128)(2,1)S(1)} %bitcast.105), channel_id=1, source_target_pairs={{0,1},{1,0},{2,3},{3,2},{4,5},{5,4},{6,7},{7,6},{8,9},{9,8},{10,11... | collective-permute-start | bytes 2359304 | tf_op jit(solution)/shard_map/ppermute | solution.py:447
  369.1 6.7 %collective-permute-start.16 = (bf16[2,2,2,16,640]{4,3,2,1,0:T(8,128)(2,1)S(1)}, bf16[2,2,2,16,640]{4,3,2,1,0:T(8,128)(2,1)S(1)}, u32[]{:S(2)}, u32[]{:S(2)}) collective-permute-start(bf16[2,2,2,16,640]{4,3,2,1,0:T(8,128)(2,1)S(1)} %dynamic-slice_bitcast_fusion.3), channel_id=1, source_target_pairs={{0,2},{1,3},{2,0},{3,1},{4,6},{5,7},{6,4},{7,5},{8,10},{9,11},{10,... | collective-permute-start | bytes 491528 | tf_op jit(solution)/shard_map/ppermute | solution.py:447
  375.9 10.1 %collective-permute-start.17 = (bf16[2,2,16,640]{3,2,1,0:T(8,128)(2,1)S(1)}, bf16[2,2,16,640]{3,2,1,0:T(8,128)(2,1)S(1)}, u32[]{:S(2)}, u32[]{:S(2)}) collective-permute-start(bf16[2,2,16,640]{3,2,1,0:T(8,128)(2,1)S(1)} %dynamic-slice_bitcast_fusion.5), channel_id=1, source_target_pairs={{0,4},{4,0},{8,12},{12,8},{16,20},{20,16},{24,28},{28,24},{1,5},{5... | collective-permute-start | bytes 245768 | tf_op jit(solution)/shard_map/ppermute | solution.py:447
  376.3 10.8 %collective-permute-start.11 = (bf16[2,2,2,16,1536]{4,3,0,1,2:T(8,128)(2,1)S(1)}, bf16[2,2,2,16,1536]{4,3,0,1,2:T(8,128)(2,1)S(1)}, u32[]{:S(2)}, u32[]{:S(2)}) collective-permute-start(bf16[2,2,2,16,1536]{4,3,0,1,2:T(8,128)(2,1)S(1)} %dynamic-slice_bitcast_fusion), channel_id=1, source_target_pairs={{0,2},{1,3},{2,0},{3,1},{4,6},{5,7},{6,4},{7,5},{8,10},{9,11},{10,... | collective-permute-start | bytes 1179656 | tf_op jit(solution)/shard_map/ppermute | solution.py:447
  386.0 4.1 collective-permute-start.18
  387.2 9.4 %collective-permute-start.12 = (bf16[2,2,16,1536]{3,2,0,1:T(8,128)(2,1)S(1)}, bf16[2,2,16,1536]{3,2,0,1:T(8,128)(2,1)S(1)}, u32[]{:S(2)}, u32[]{:S(2)}) collective-permute-start(bf16[2,2,16,1536]{3,2,0,1:T(8,128)(2,1)S(1)} %dynamic-slice_bitcast_fusion.2), channel_id=1, source_target_pairs={{0,4},{4,0},{8,12},{12,8},{16,20},{20,16},{24,28},{28,24},{1,5},{5... | collective-permute-start | bytes 589832 | tf_op jit(solution)/shard_map/ppermute | solution.py:447
  390.1 8.6 %collective-permute-start.19 = (bf16[16,640]{1,0:T(8,128)(2,1)S(1)}, bf16[16,640]{1,0:T(8,128)(2,1)S(1)}, u32[]{:S(2)}, u32[]{:S(2)}) collective-permute-start(bf16[16,640]{1,0:T(8,128)(2,1)S(1)} %dynamic-slice_bitcast_fusion.8), channel_id=1, source_target_pairs={{0,16},{4,20},{8,24},{12,28},{16,0},{20,4},{24,8},{28,12},{1,17},{... | collective-permute-start | bytes 61448 | tf_op jit(solution)/shard_map/ppermute | solution.py:447
  392.6 22.6 %all-to-all-start.4 = ((bf16[4,64,2048]{2,1,0:T(8,128)(2,1)}), bf16[4,64,2048]{2,1,0:T(8,128)(2,1)S(1)}, u32[]{:S(2)}, u32[]{:S(2)}) async-start(bf16[4,64,2048]{2,1,0:T(8,128)(2,1)} %bitcast.43), calls=%async_computation.4 | async-start | bytes 2097152 | tf_op jit(solution)/shard_map/all_to_all | solution.py:509
  396.6 13.5 %collective-permute-start.13 = (bf16[2,16,1536]{2,1,0:T(8,128)(2,1)S(1)}, bf16[2,16,1536]{2,1,0:T(8,128)(2,1)S(1)}, u32[]{:S(2)}, u32[]{:S(2)}) collective-permute-start(bf16[2,16,1536]{2,1,0:T(8,128)(2,1)S(1)} %dynamic-slice_bitcast_fusion.4), channel_id=1, source_target_pairs={{0,8},{4,12},{8,0},{12,4},{16,24},{20,28},{24,16},{28,20},{1,9},{5... | collective-permute-start | bytes 294920 | tf_op jit(solution)/shard_map/ppermute | solution.py:447
  410.2 6.7 %collective-permute-start.14 = (bf16[16,1536]{1,0:T(8,128)(2,1)S(1)}, bf16[16,1536]{1,0:T(8,128)(2,1)S(1)}, u32[]{:S(2)}, u32[]{:S(2)}) collective-permute-start(bf16[16,1536]{1,0:T(8,128)(2,1)S(1)} %dynamic-slice_bitcast_fusion.6), channel_id=1, source_target_pairs={{0,16},{4,20},{8,24},{12,28},{16,0},{20,4},{24,8},{28,12},{1,17},{... | collective-permute-start | bytes 147464 | tf_op jit(solution)/shard_map/ppermute | solution.py:447
  415.3 1.6 copy-start.4
  (1 other events, 1.0 us)
